TPU v7x, 32 devices: a whole 2x2x4 slice. The times are simulated.
32 devices in a mesh: grp: 4 (over z), tok: 8 (over y, x, core).
Axes of the slice: x: 2, y: 2, z: 4, core: 2. Of those that a mesh axis runs over, the one named last changes fastest.
Arguments:
- tokens: bfloat16 [4, 2, 8192, 512], P('grp', None, 'tok'), may hold values from -6 to 6
- latents: float32 [4, 2, 2048, 512], P('grp'), may hold values from -6 to 6
- segments: int32 [4, 2, 8192], P('grp', None, 'tok'), may hold values from 0 to 7, as said below
- scene_mask: int32 [4, 2, 8, 8], P('grp'), may hold values from 0 to 1
- counts: int32 [4, 2, 8], P('grp', None, 'tok'), may hold values from 512 to 1024, as said below
- token_gain: float32 [512], replicated, may hold values from 0.1 to 1.9
- query_gain: float32 [512], replicated, may hold values from 0.1 to 1.9
- query_weight: bfloat16 [512, 512], replicated, may hold values from -0.5 to 0.5
- key_weight: bfloat16 [512, 512], replicated, may hold values from -0.25 to 0.25
- value_weight: bfloat16 [512, 512], replicated, may hold values from -0.25 to 0.25
- output_weight: bfloat16 [512, 512], replicated, may hold values from -4 to 4
- first_gain: float32 [512], replicated, may hold values from 0.1 to 1.9
- first_up: bfloat16 [512, 2048], replicated, may hold values from -0.25 to 0.25
- first_down: bfloat16 [2048, 512], replicated, may hold values from -0.25 to 0.25
- mixer_gain: float32 [512], replicated, may hold values from 0.1 to 1.9
- mixer_project: bfloat16 [512, 1536], replicated, may hold values from -0.25 to 0.25
- mixer_output: bfloat16 [512, 512], replicated, may hold values from -6 to 6
- second_gain: float32 [512], replicated, may hold values from 0.1 to 1.9
- second_up: bfloat16 [512, 2048], replicated, may hold values from -0.25 to 0.25
- second_down: bfloat16 [2048, 512], replicated, may hold values from -0.25 to 0.25
- cotangent: float32 [4, 2, 2048, 512], P('grp', None, 'tok'), may hold values from -6 to 6
Outputs:
- latents_out: float32 [4, 2, 2048, 512], P('grp', None, 'tok')
- latents_grad: float32 [4, 2, 2048, 512], P('grp', None, 'tok')
- tokens_grad: float32 [4, 2, 8192, 512], P('grp', None, 'tok')
- grad_token_gain: float32 [512], P('tok')
- grad_query_gain: float32 [512], P('tok')
- grad_query_weight: float32 [512, 512], P('tok')
- grad_key_weight: float32 [512, 512], P('tok')
- grad_value_weight: float32 [512, 512], P('tok')
- grad_output_weight: float32 [512, 512], P('tok')
- grad_first_gain: float32 [512], P('tok')
- grad_first_up: float32 [512, 2048], P('tok')
- grad_first_down: float32 [2048, 512], P('tok')
- grad_mixer_gain: float32 [512], P('tok')
- grad_mixer_project: float32 [512, 1536], P('tok')
- grad_mixer_output: float32 [512, 512], P('tok')
- grad_second_gain: float32 [512], P('tok')
- grad_second_up: float32 [512, 2048], P('tok')
- grad_second_down: float32 [2048, 512], P('tok')
Inputs may be any that keep to these rules, and one draw needn't show every extreme that they name: `segments`: scenes come in runs of 32 tokens; in every set one scene holds the first 32 tokens of every device's share, and every latent group sees it. The first counts tokens of a device's share of a set are live, the rest are padding that no latent sees; in every set some device is full.
All inputs are finite; a program needn't handle non-finite values.
Results may differ from a plain program's by a relative error of at most 0.034.
Values may be sent and summed in bfloat16 or wider, within the bound.
A program may use at most 256 MiB of HBM per device.

v0:
```python
import jax
import jax.numpy as jnp
from jax import lax
from jax.sharding import PartitionSpec as P

D = 512
L = 2048
H = 8
HD = 64
TOK_DEV = 1024
MB = 2
SCENES = 8
LGROUPS = 8


EPS = 1e-05
NEG = -1e30


def norm_rows(values, gain):
    centre = values - jnp.mean(values, axis=-1, keepdims=True)
    spread = jnp.mean(centre * centre, axis=-1, keepdims=True)
    return centre * lax.rsqrt(spread + EPS) * gain


def norm_back(values, gain, upstream):
    unused, pull = jax.vjp(norm_rows, values, gain)
    return pull(upstream)


def gelu_back(hidden, upstream):
    unused, pull = jax.vjp(jax.nn.gelu, hidden)
    return pull(upstream)[0]


def product_plain(left, right):
    return jnp.dot(left, right, preferred_element_type=jnp.float32)


def product_rows(left, right):
    return lax.dot_general(
        left, right, (((0,), (0,)), ((), ())), preferred_element_type=jnp.float32
    )


def product_cols(left, right):
    return lax.dot_general(
        left, right, (((1,), (1,)), ((), ())), preferred_element_type=jnp.float32
    )


def add_term(store, name, value):
    if name in store:
        store[name] = store[name] + value
    else:
        store[name] = value


def project_tokens(tokens, member, token_gain, key_weight, value_weight):
    source = tokens[0, member].astype(jnp.float32)
    normed = norm_rows(source, token_gain).astype(jnp.bfloat16)
    key_rows = product_plain(normed, key_weight).astype(jnp.bfloat16)
    value_rows = product_plain(normed, value_weight).astype(jnp.bfloat16)
    return (source, normed, key_rows, value_rows)


def mlp_forward(residual, gain, up_weight, down_weight):
    normed = norm_rows(residual, gain).astype(jnp.bfloat16)
    hidden = product_plain(normed, up_weight)
    active = jax.nn.gelu(hidden).astype(jnp.bfloat16)
    return (residual + product_plain(active, down_weight), (normed, hidden, active))


def mlp_backward(residual, gain, up_weight, down_weight, saved, upstream):
    normed, hidden, active = saved
    grad_low = upstream.astype(jnp.bfloat16)
    grad_down = product_rows(active, grad_low)
    hidden_grad = gelu_back(hidden, product_cols(grad_low, down_weight)).astype(jnp.bfloat16)
    grad_up = product_rows(normed, hidden_grad)
    residual_grad, grad_gain = norm_back(residual, gain, product_cols(hidden_grad, up_weight))
    return (upstream + residual_grad, grad_gain, grad_up, grad_down)


def mixer_forward(residual, gain, project, output):
    own_rows = residual.shape[0]
    normed = norm_rows(residual, gain).astype(jnp.bfloat16)
    packed = product_plain(normed, project).astype(jnp.bfloat16)
    pair_rows = lax.all_gather(packed[:, D:], "tok", axis=0, tiled=True)
    every = pair_rows.shape[0]
    own_queries = packed[:, :D].reshape(own_rows, H, HD)
    keys = pair_rows[:, :D].reshape(every, H, HD)
    values = pair_rows[:, D:].reshape(every, H, HD)
    logits = jnp.einsum(
        "qhd,khd->hqk", own_queries, keys, preferred_element_type=jnp.float32
    ) * HD ** (-0.5)
    peak_row = jnp.max(logits, axis=-1, keepdims=True)
    raised = jnp.exp(logits - peak_row)
    softened = raised / jnp.sum(raised, axis=-1, keepdims=True)
    softened_low = softened.astype(jnp.bfloat16)
    mixed_rows = jnp.einsum(
        "hqk,khd->qhd", softened_low, values, preferred_element_type=jnp.float32
    )
    mixed_rows = mixed_rows.reshape(own_rows, D).astype(jnp.bfloat16)
    return (
        residual + product_plain(mixed_rows, output),
        (normed, own_queries, keys, values, softened, softened_low, mixed_rows),
    )


def mixer_backward(residual, gain, project, output, saved, upstream):
    normed, own_queries, keys, values, softened, softened_low, mixed_rows = saved
    own_rows = upstream.shape[0]
    every = keys.shape[0]
    grad_low = upstream.astype(jnp.bfloat16)
    grad_output = product_rows(mixed_rows, grad_low)
    mixed_grad = product_cols(grad_low, output).astype(jnp.bfloat16).reshape(own_rows, H, HD)
    value_grad = jnp.einsum(
        "hqk,qhd->khd", softened_low, mixed_grad, preferred_element_type=jnp.float32
    )
    soft_grad = jnp.einsum("qhd,khd->hqk", mixed_grad, values, preferred_element_type=jnp.float32)
    logit_grad = softened * (soft_grad - jnp.sum(soft_grad * softened, axis=-1, keepdims=True))
    logit_grad = logit_grad.astype(jnp.bfloat16)
    query_grad = jnp.einsum(
        "hqk,khd->qhd", logit_grad, keys, preferred_element_type=jnp.float32
    ) * HD ** (-0.5)
    key_grad = jnp.einsum(
        "hqk,qhd->khd", logit_grad, own_queries, preferred_element_type=jnp.float32
    ) * HD ** (-0.5)
    pair_terms = jnp.concatenate([key_grad.reshape(every, D), value_grad.reshape(every, D)], axis=1)
    pair_grad = lax.psum_scatter(
        pair_terms.astype(jnp.bfloat16), "tok", scatter_dimension=0, tiled=True
    ).astype(jnp.float32)
    packed_grad = jnp.concatenate([query_grad.reshape(own_rows, D), pair_grad], axis=1).astype(
        jnp.bfloat16
    )
    grad_project = product_rows(normed, packed_grad)
    residual_grad, grad_gain = norm_back(residual, gain, product_cols(packed_grad, project))
    return (upstream + residual_grad, grad_gain, grad_project, grad_output)


def body(
    tokens,
    latents,
    segments,
    scene_mask,
    counts,
    token_gain,
    query_gain,
    query_weight,
    key_weight,
    value_weight,
    output_weight,
    first_gain,
    first_up,
    first_down,
    mixer_gain,
    mixer_project,
    mixer_output,
    second_gain,
    second_up,
    second_down,
    cotangent,
):
    scale = D ** (-0.5)
    shards = lax.axis_size("tok")
    own_rows = L // shards
    row_start = lax.axis_index("tok") * own_rows
    latent_group = jnp.arange(L) // (L // LGROUPS)
    latent_onehot = (latent_group[:, None] == jnp.arange(LGROUPS)[None, :]).astype(jnp.float32)
    token_place = jnp.arange(TOK_DEV)
    records = []
    latent_outs = []
    for member in range(MB):
        record = {}
        source, normed, key_rows, value_rows = project_tokens(
            tokens, member, token_gain, key_weight, value_weight
        )
        record["token_side"] = (source, normed, key_rows, value_rows)
        scene_onehot = (segments[0, member][:, None] == jnp.arange(SCENES)[None, :]).astype(
            jnp.float32
        )
        token_seen = jnp.dot(scene_onehot, scene_mask[0, member].astype(jnp.float32))
        visible = product_cols(latent_onehot, token_seen)
        alive = token_place < counts[0, member, 0]
        allowed = (visible > 0.5) & alive[None, :]
        latent_every = latents[0, member]
        normed_every = norm_rows(latent_every, query_gain).astype(jnp.bfloat16)
        queries = product_plain(normed_every, query_weight).astype(jnp.bfloat16)
        scores = jnp.where(allowed, product_cols(queries, key_rows) * scale, NEG)
        row_top = lax.pmax(jnp.max(scores, axis=1), "tok")
        unnormed = jnp.exp(scores - row_top[:, None])
        row_total, weighted = (
            lax.psum_scatter(
                jnp.sum(unnormed, axis=1).astype(jnp.bfloat16),
                "tok",
                scatter_dimension=0,
                tiled=True,
            ).astype(jnp.float32),
            lax.psum_scatter(
                product_plain(unnormed.astype(jnp.bfloat16), value_rows).astype(jnp.bfloat16),
                "tok",
                scatter_dimension=0,
                tiled=True,
            ).astype(jnp.float32),
        )
        latent_in = lax.dynamic_slice_in_dim(latent_every, row_start, own_rows, 0)
        latent_normed = lax.dynamic_slice_in_dim(normed_every, row_start, own_rows, 0)
        attended = weighted / row_total[:, None]
        attended_low = attended.astype(jnp.bfloat16)
        first_mid = latent_in + product_plain(attended_low, output_weight)
        mixer_mid, first_saved = mlp_forward(first_mid, first_gain, first_up, first_down)
        second_mid, mixer_saved = mixer_forward(mixer_mid, mixer_gain, mixer_project, mixer_output)
        final_rows, second_saved = mlp_forward(second_mid, second_gain, second_up, second_down)
        latent_outs.append(final_rows)
        record["latent_side"] = (
            allowed,
            latent_in,
            latent_normed,
            queries,
            row_top,
            row_total,
            attended,
            attended_low,
            first_mid,
            mixer_mid,
            second_mid,
            first_saved,
            mixer_saved,
            second_saved,
        )
        records.append(record)
    grads = {}
    latent_grads = []
    token_grads = []
    for member in range(MB):
        record = records[member]
        source, normed, key_rows, value_rows = record["token_side"]
        (
            allowed,
            latent_in,
            latent_normed,
            queries,
            row_top,
            row_total,
            attended,
            attended_low,
            first_mid,
            mixer_mid,
            second_mid,
            first_saved,
            mixer_saved,
            second_saved,
        ) = record["latent_side"]
        second_back = mlp_backward(
            second_mid, second_gain, second_up, second_down, second_saved, cotangent[0, member]
        )
        add_term(grads, "second_gain", second_back[1])
        add_term(grads, "second_up", second_back[2])
        add_term(grads, "second_down", second_back[3])
        mixer_back = mixer_backward(
            mixer_mid, mixer_gain, mixer_project, mixer_output, mixer_saved, second_back[0]
        )
        add_term(grads, "mixer_gain", mixer_back[1])
        add_term(grads, "mixer_project", mixer_back[2])
        add_term(grads, "mixer_output", mixer_back[3])
        first_back = mlp_backward(
            first_mid, first_gain, first_up, first_down, first_saved, mixer_back[0]
        )
        add_term(grads, "first_gain", first_back[1])
        add_term(grads, "first_up", first_back[2])
        add_term(grads, "first_down", first_back[3])
        latent_upstream = first_back[0]
        grad_low = latent_upstream.astype(jnp.bfloat16)
        add_term(grads, "output_weight", product_rows(attended_low, grad_low))
        attended_grad = lax.optimization_barrier(
            product_cols(grad_low, output_weight).astype(jnp.bfloat16)
        ).astype(jnp.float32)
        weighted_grad = (attended_grad / row_total[:, None]).astype(jnp.bfloat16)
        total_grad = -jnp.sum(attended_grad * attended, axis=1) / row_total
        weighted_every, total_every = (
            lax.all_gather(
                weighted_grad.astype(jnp.float32).astype(jnp.bfloat16), "tok", axis=0, tiled=True
            ).astype(jnp.float32),
            lax.all_gather(total_grad.astype(jnp.bfloat16), "tok", axis=0, tiled=True).astype(
                total_grad.dtype
            ),
        )
        weighted_every = weighted_every.astype(jnp.bfloat16)
        scores = jnp.where(allowed, product_cols(queries, key_rows) * scale, NEG)
        unnormed = jnp.exp(scores - row_top[:, None])
        unnormed_grad = product_cols(weighted_every, value_rows) + total_every[:, None]
        score_grad = (unnormed * unnormed_grad).astype(jnp.bfloat16)
        value_grad = product_rows(unnormed.astype(jnp.bfloat16), weighted_every).astype(
            jnp.bfloat16
        )
        key_grad = (product_rows(score_grad, queries) * scale).astype(jnp.bfloat16)
        query_grad = lax.psum_scatter(
            (product_plain(score_grad, key_rows) * scale).astype(jnp.bfloat16),
            "tok",
            scatter_dimension=0,
            tiled=True,
        )
        add_term(grads, "key_weight", product_rows(normed, key_grad))
        add_term(grads, "value_weight", product_rows(normed, value_grad))
        normed_grad = product_cols(key_grad, key_weight) + product_cols(value_grad, value_weight)
        source_grad, gain_grad = norm_back(source, token_gain, normed_grad)
        add_term(grads, "token_gain", gain_grad)
        token_grads.append(source_grad)
        add_term(grads, "query_weight", product_rows(latent_normed, query_grad))
        latent_grad, gain_grad = norm_back(
            latent_in, query_gain, product_cols(query_grad, query_weight)
        )
        add_term(grads, "query_gain", gain_grad)
        latent_grads.append(latent_upstream + latent_grad)
    parts = (
        lax.psum_scatter(
            grads["token_gain"].astype(jnp.bfloat16), "tok", scatter_dimension=0, tiled=True
        ).astype(jnp.float32),
        lax.psum_scatter(
            grads["query_gain"].astype(jnp.bfloat16), "tok", scatter_dimension=0, tiled=True
        ).astype(jnp.float32),
        lax.psum_scatter(
            grads["query_weight"].astype(jnp.bfloat16), "tok", scatter_dimension=0, tiled=True
        ).astype(jnp.float32),
        lax.psum_scatter(
            grads["key_weight"].astype(jnp.bfloat16), "tok", scatter_dimension=0, tiled=True
        ).astype(jnp.float32),
        lax.psum_scatter(
            grads["value_weight"].astype(jnp.bfloat16), "tok", scatter_dimension=0, tiled=True
        ).astype(jnp.float32),
        lax.psum_scatter(
            grads["output_weight"].astype(jnp.bfloat16), "tok", scatter_dimension=0, tiled=True
        ).astype(jnp.float32),
        lax.psum_scatter(
            grads["first_gain"].astype(jnp.bfloat16), "tok", scatter_dimension=0, tiled=True
        ).astype(jnp.float32),
        lax.psum_scatter(
            grads["first_up"].astype(jnp.bfloat16), "tok", scatter_dimension=0, tiled=True
        ).astype(jnp.float32),
        lax.psum_scatter(
            grads["first_down"].astype(jnp.bfloat16), "tok", scatter_dimension=0, tiled=True
        ).astype(jnp.float32),
        lax.psum_scatter(
            grads["mixer_gain"].astype(jnp.bfloat16), "tok", scatter_dimension=0, tiled=True
        ).astype(jnp.float32),
        lax.psum_scatter(
            grads["mixer_project"].astype(jnp.bfloat16), "tok", scatter_dimension=0, tiled=True
        ).astype(jnp.float32),
        lax.psum_scatter(
            grads["mixer_output"].astype(jnp.bfloat16), "tok", scatter_dimension=0, tiled=True
        ).astype(jnp.float32),
        lax.psum_scatter(
            grads["second_gain"].astype(jnp.bfloat16), "tok", scatter_dimension=0, tiled=True
        ).astype(jnp.float32),
        lax.psum_scatter(
            grads["second_up"].astype(jnp.bfloat16), "tok", scatter_dimension=0, tiled=True
        ).astype(jnp.float32),
        lax.psum_scatter(
            grads["second_down"].astype(jnp.bfloat16), "tok", scatter_dimension=0, tiled=True
        ).astype(jnp.float32),
    )
    summed = (
        lax.psum(parts[0].astype(jnp.bfloat16), "grp").astype(jnp.float32),
        lax.psum(parts[1].astype(jnp.bfloat16), "grp").astype(jnp.float32),
        lax.psum(parts[2].astype(jnp.bfloat16), "grp").astype(jnp.float32),
        lax.psum(parts[3].astype(jnp.bfloat16), "grp").astype(jnp.float32),
        lax.psum(parts[4].astype(jnp.bfloat16), "grp").astype(jnp.float32),
        lax.psum(parts[5].astype(jnp.bfloat16), "grp").astype(jnp.float32),
        lax.psum(parts[6].astype(jnp.bfloat16), "grp").astype(jnp.float32),
        lax.psum(parts[7].astype(jnp.bfloat16), "grp").astype(jnp.float32),
        lax.psum(parts[8].astype(jnp.bfloat16), "grp").astype(jnp.float32),
        lax.psum(parts[9].astype(jnp.bfloat16), "grp").astype(jnp.float32),
        lax.psum(parts[10].astype(jnp.bfloat16), "grp").astype(jnp.float32),
        lax.psum(parts[11].astype(jnp.bfloat16), "grp").astype(jnp.float32),
        lax.psum(parts[12].astype(jnp.bfloat16), "grp").astype(jnp.float32),
        lax.psum(parts[13].astype(jnp.bfloat16), "grp").astype(jnp.float32),
        lax.psum(parts[14].astype(jnp.bfloat16), "grp").astype(jnp.float32),
    )
    return (
        jnp.stack(latent_outs)[None],
        jnp.stack(latent_grads)[None],
        jnp.stack(token_grads)[None],
    ) + tuple(summed)


def solution(mesh):
    return jax.shard_map(
        body,
        mesh=mesh,
        in_specs=(
            P("grp", None, "tok", None),
            P("grp", None, None, None),
            P("grp", None, "tok"),
            P("grp", None, None, None),
            P("grp", None, "tok"),
            P(),
            P(),
            P(),
            P(),
            P(),
            P(),
            P(),
            P(),
            P(),
            P(),
            P(),
            P(),
            P(),
            P(),
            P(),
            P("grp", None, "tok", None),
        ),
        out_specs=(
            P("grp", None, "tok", None),
            P("grp", None, "tok", None),
            P("grp", None, "tok", None),
            P("tok"),
            P("tok"),
            P("tok", None),
            P("tok", None),
            P("tok", None),
            P("tok", None),
            P("tok"),
            P("tok", None),
            P("tok", None),
            P("tok"),
            P("tok", None),
            P("tok", None),
            P("tok"),
            P("tok", None),
            P("tok", None),
        ),
        check_vma=False,
    )
```

profile of v0, /device:TPU:0, one launch (start us, length us, event | category | flops | bytes accessed | tf_op | source)
XLA Modules:
  0.0 1121.2 jit_solution(5326714692897680441)
XLA Ops:
  18.3 7.7 slice_reduce_fusion.1
  40.4 4.8 fusion.98
  45.1 4.8 fusion.101
  53.7 10.5 fusion.220
  64.2 5.3 fusion.221
  69.5 25.8 %all-reduce.7 = (f32[2048]{0:T(1024)S(1)}, f32[2048]{0:T(1024)S(1)}) all-reduce(f32[2048]{0:T(1024)S(1)} %get-tuple-element.173, f32[2048]{0:T(1024)S(1)} %get-tuple-element.175), channel_id=1, replica_groups=mesh['grp'=4,'tok'=8] {'tok'}, use_global_device_ids=true, to_apply=%region_22.23 | all-reduce | flops 4096 | bytes 32768 | tf_op jit(solution)/shard_map/pmax | solution.py:190
  95.4 7.4 convolution_convert_fusion.1
  106.8 7.5 convolution_convert_fusion
  114.4 4.6 fusion.12
  120.3 4.8 fusion.10
  125.1 12.4 %all-reduce.9 = (bf16[2048]{0:T(1024)(128)(2,1)S(1)}, bf16[2048]{0:T(1024)(128)(2,1)S(1)}) all-reduce(bf16[2048]{0:T(1024)(128)(2,1)S(1)} %fusion.12, bf16[2048]{0:T(1024)(128)(2,1)S(1)} %fusion.10), channel_id=5, replica_groups=mesh['grp'=4,'tok'=8] {'tok'}, use_global_device_ids=true, to_apply=%region_25.26.clone | all-reduce | flops 4096 | bytes 16384
  137.7 6.2 reduce-scatter.17.cloned.1.call-done
  153.8 35.5 %reduce-scatter.19.cloned.1.call-done = bf16[256,512]{1,0:T(8,128)(2,1)} async-done(((bf16[2048,512]{1,0:T(8,128)(2,1)}), bf16[256,512]{1,0:T(8,128)(2,1)}) %reduce-scatter.19.cloned.1.call-update) | async-done | bytes 262160 | tf_op jit(solution)/shard_map/reduce_scatter | solution.py:199
  200.3 28.2 %all-gather.7.cloned.1.call-done = bf16[2048,1024]{1,0:T(8,128)(2,1)} async-done(((bf16[256,1024]{1,0:T(8,128)(2,1)}), bf16[2048,1024]{1,0:T(8,128)(2,1)}) %all-gather.7.cloned.1.call-update) | async-done | bytes 4194320 | tf_op jit(solution)/shard_map/all_gather | solution.py:88
  228.5 4.7 fusion.215
  241.2 9.6 fusion.228
  250.8 9.9 fusion.92
  261.6 6.0 all-gather.9.cloned.1.call-done
  280.0 9.7 fusion.224
  289.8 9.2 fusion.95
  310.8 11.4 %multiply_reduce_fusion = (f32[8,256]{1,0:T(8,128)S(1)}, f32[8,256,2048]{2,1,0:T(8,128)}) fusion(f32[8,256,2048]{2,1,0:T(8,128)} %get-tuple-element.182, f32[8,256]{1,0:T(8,128)S(1)} %get-tuple-element.181, bf16[256,8,64]{0,2,1:T(8,128)(2,1)S(1)} %bitcast.329, bf16[2048,8,64]{0,2,1:T(8,128)(2,1)} %bitcast.312), kind=kOutput, calls=%fused_computation.3 | convolution fusion | flops 549451776 | bytes 35930112 | tf_op jit(solution)/shard_map/qhd,khd->hqk/dot_general | solution.py:120
  322.3 8.8 fusion.25
  332.2 11.5 %multiply_convert_fusion = bf16[8,256,2048]{2,1,0:T(8,128)(2,1)S(1)} fusion(f32[8,256,2048]{2,1,0:T(8,128)} %get-tuple-element.197, f32[8,256]{1,0:T(8,128)S(1)} %get-tuple-element.196, f32[8,256,2048]{2,1,0:T(8,128)} %get-tuple-element.182, f32[8,256]{1,0:T(8,128)S(1)} %get-tuple-element.181), kind=kLoop, calls=%fused_computation.2 | loop fusion | flops 16777216 | bytes 41959424 | tf_op jit(solution)/shard_map/convert_element_type | solution.py:122
  351.6 14.0 %multiply_reduce_fusion.1 = (f32[8,256]{1,0:T(8,128)S(1)}, f32[8,256,2048]{2,1,0:T(8,128)}) fusion(f32[8,256,2048]{2,1,0:T(8,128)} %get-tuple-element.190, f32[8,256]{1,0:T(8,128)S(1)} %get-tuple-element.189, bf16[256,8,64]{0,2,1:T(8,128)(2,1)} %bitcast.327, bf16[2048,8,64]{0,2,1:T(8,128)(2,1)S(1)} %bitcast.310), kind=kOutput, calls=%fused_computation.5 | convolution fusion | flops 549451776 | bytes 35930112 | tf_op jit(solution)/shard_map/qhd,khd->hqk/dot_general | solution.py:120
  368.5 7.7 multiply_convert_fusion.1
  387.2 6.2 fusion.90
  393.4 6.1 fusion.91
  403.8 52.7 %reduce-scatter.21.cloned.1.call-done = bf16[256,1024]{0,1:T(8,128)(2,1)} async-done(((bf16[2048,1024]{0,1:T(8,128)(2,1)}), bf16[256,1024]{0,1:T(8,128)(2,1)}) %reduce-scatter.21.cloned.1.call-update) | async-done | bytes 524304 | tf_op jit(solution)/shard_map/reduce_scatter | solution.py:130
  478.5 8.8 all-gather
  487.3 13.0 %all-gather.11.cloned.1.call-done = bf16[2048,512]{1,0:T(8,128)(2,1)} async-done(((bf16[256,512]{1,0:T(8,128)(2,1)}), bf16[2048,512]{1,0:T(8,128)(2,1)}) %all-gather.11.cloned.1.call-update) | async-done | bytes 2097168 | tf_op jit(solution)/shard_map/all_gather | solution.py:281
  500.2 6.9 multiply_convert_fusion.3
  513.8 8.8 all-gather.1
  522.6 7.4 all-gather.13.cloned.1.call-done
  530.1 6.9 multiply_convert_fusion.2
  586.2 4.9 multiply_convert_fusion.11
  617.7 5.4 copy.85
  630.1 13.5 %all-reduce.8 = (bf16[512]{0:T(512)(128)(2,1)S(1)}, bf16[512]{0:T(512)(128)(2,1)S(1)}, bf16[512]{0:T(512)(128)(2,1)S(1)}, bf16[512]{0:T(512)(128)(2,1)S(1)}, bf16[512]{0:T(512)(128)(2,1)S(1)}) all-reduce(bf16[512]{0:T(512)(128)(2,1)S(1)} %add_convert_fusion.8, ...), channel_id=10, replica_groups=mesh['grp'=4,'tok'=8] {'tok'}, use_global_device_ids=true, to_apply=%region_68.69.clone | all-reduce | flops 2560 | bytes 10240
  644.1 11.7 %all-reduce.10 = (bf16[64]{0:T(256)(128)(2,1)S(1)}, bf16[64]{0:T(256)(128)(2,1)S(1)}, bf16[64]{0:T(256)(128)(2,1)S(1)}, bf16[64]{0:T(256)(128)(2,1)S(1)}, bf16[64]{0:T(256)(128)(2,1)S(1)}) all-reduce(bf16[64]{0:T(256)(128)(2,1)S(1)} %dynamic-slice.7, bf16[64]{0:T(256)(128)(2,1)S(1)} %dynamic-slice.9, ...), channel_id=1, replica_groups=mesh['grp'=4,'tok'=8] {'grp'}, use_global_device_ids=true, to_apply=%region_69.70 | all-reduce | flops 320 | bytes 1280 | tf_op jit(solution)/shard_map/psum | solution.py:363
  658.3 43.1 %reduce-scatter.45.cloned.1.call-done = bf16[64,2048]{1,0:T(8,128)(2,1)} async-done(((bf16[512,2048]{1,0:T(8,128)(2,1)}), bf16[64,2048]{1,0:T(8,128)(2,1)}) %reduce-scatter.45.cloned.1.call-update) | async-done | bytes 262160 | tf_op jit(solution)/shard_map/reduce_scatter | solution.py:355
  701.4 44.5 %reduce-scatter.47.cloned.1.call-done = bf16[256,512]{1,0:T(8,128)(2,1)} async-done(((bf16[2048,512]{1,0:T(8,128)(2,1)}), bf16[256,512]{1,0:T(8,128)(2,1)}) %reduce-scatter.47.cloned.1.call-update) | async-done | bytes 262160 | tf_op jit(solution)/shard_map/reduce_scatter | solution.py:358
  745.9 37.4 %reduce-scatter.35.cloned.1.call-done = bf16[64,512]{1,0:T(8,128)(2,1)} async-done(((bf16[512,512]{1,0:T(8,128)(2,1)}), bf16[64,512]{1,0:T(8,128)(2,1)}) %reduce-scatter.35.cloned.1.call-update) | async-done | bytes 65552 | tf_op jit(solution)/shard_map/reduce_scatter | solution.py:331
  783.3 41.6 %reduce-scatter.41.cloned.1.call-done = bf16[64,1536]{1,0:T(8,128)(2,1)} async-done(((bf16[512,1536]{1,0:T(8,128)(2,1)}), bf16[64,1536]{1,0:T(8,128)(2,1)}) %reduce-scatter.41.cloned.1.call-update) | async-done | bytes 196624 | tf_op jit(solution)/shard_map/reduce_scatter | solution.py:346
  824.9 44.4 %reduce-scatter.39.cloned.1.call-done = bf16[256,512]{1,0:T(8,128)(2,1)} async-done(((bf16[2048,512]{1,0:T(8,128)(2,1)}), bf16[256,512]{1,0:T(8,128)(2,1)}) %reduce-scatter.39.cloned.1.call-update) | async-done | bytes 262160 | tf_op jit(solution)/shard_map/reduce_scatter | solution.py:340
  869.3 44.8 %reduce-scatter.37.cloned.1.call-done = bf16[64,2048]{1,0:T(8,128)(2,1)} async-done(((bf16[512,2048]{1,0:T(8,128)(2,1)}), bf16[64,2048]{1,0:T(8,128)(2,1)}) %reduce-scatter.37.cloned.1.call-update) | async-done | bytes 262160 | tf_op jit(solution)/shard_map/reduce_scatter | solution.py:337
  914.1 37.7 %reduce-scatter.33.cloned.1.call-done = bf16[64,512]{1,0:T(8,128)(2,1)} async-done(((bf16[512,512]{1,0:T(8,128)(2,1)}), bf16[64,512]{1,0:T(8,128)(2,1)}) %reduce-scatter.33.cloned.1.call-update) | async-done | bytes 65552 | tf_op jit(solution)/shard_map/reduce_scatter | solution.py:328
  951.7 38.1 %reduce-scatter.31.cloned.1.call-done = bf16[64,512]{1,0:T(8,128)(2,1)} async-done(((bf16[512,512]{1,0:T(8,128)(2,1)}), bf16[64,512]{1,0:T(8,128)(2,1)}) %reduce-scatter.31.cloned.1.call-update) | async-done | bytes 65552 | tf_op jit(solution)/shard_map/reduce_scatter | solution.py:325
  989.9 37.6 %reduce-scatter.29.cloned.1.call-done = bf16[64,512]{1,0:T(8,128)(2,1)} async-done(((bf16[512,512]{1,0:T(8,128)(2,1)}), bf16[64,512]{1,0:T(8,128)(2,1)}) %reduce-scatter.29.cloned.1.call-update) | async-done | bytes 65552 | tf_op jit(solution)/shard_map/reduce_scatter | solution.py:322
  1030.2 73.4 %all-reduce.14.cloned.1.call-done = (bf16[64,512]{1,0:T(8,128)(2,1)}, bf16[64,512]{1,0:T(8,128)(2,1)}, bf16[64,512]{1,0:T(8,128)(2,1)}, bf16[64,512]{1,0:T(8,128...) async-done(((bf16[64,512]{1,0:T(8,128)(2,1)}, ...) | async-done | bytes 1572880 | tf_op jit(solution)/shard_map/psum | solution.py:365
  (664 shorter events, 239.6 us)
Async XLA Ops:
  7.2 292.5 %copy-start = (bf16[512,2048]{1,0:T(8,128)(2,1)S(1)}, bf16[512,2048]{1,0:T(8,128)(2,1)}, u32[]{:S(2)}) copy-start(bf16[512,2048]{1,0:T(8,128)(2,1)} %param.39) | copy-start | bytes 6291460
  7.2 136.7 %reduce-scatter.17.cloned.1.call-start = ((), (), s32[]{:S(2)}) async-start(), calls=%async_computation.16 | async-start | bytes 2359296 | tf_op jit(solution)/shard_map/reduce_scatter | solution.py:199
  11.9 38.8 %copy-start.4 = (bf16[1,1,1024,512]{2,3,1,0:T(8,128)(2,1)}, bf16[1,1,1024,512]{2,3,1,0:T(8,128)(2,1)S(1)}, u32[]{:S(2)}) copy-start(bf16[1,1,1024,512]{2,3,1,0:T(8,128)(2,1)S(1)} %copy.88) | copy-start | bytes 3145732
  12.1 38.6 %copy-start.109 = (f32[1024]{0:T(1024)}, f32[1024]{0:T(1024)S(1)}, u32[]{:S(2)}) copy-start(f32[1024]{0:T(1024)S(1)} %broadcast_multiply_fusion.3) | copy-start | bytes 12292
  16.1 34.6 %copy-start.150 = (f32[1024]{0:T(1024)}, f32[1024]{0:T(1024)S(1)}, u32[]{:S(2)}) copy-start(f32[1024]{0:T(1024)S(1)} %get-tuple-element.207) | copy-start | bytes 12292
  16.1 86.7 %copy-start.111 = (f32[1024]{0:T(1024)}, f32[1024]{0:T(1024)S(1)}, u32[]{:S(2)}) copy-start(f32[1024]{0:T(1024)S(1)} %get-tuple-element.208) | copy-start | bytes 12292
  18.3 84.5 %copy-start.132 = (f32[1024]{0:T(1024)}, f32[1024]{0:T(1024)S(1)}, u32[]{:S(2)}) copy-start(f32[1024]{0:T(1024)S(1)} %fusion.168) | copy-start | bytes 12292
  95.3 19.1 %copy-start.161 = (f32[2048]{0:T(1024)}, f32[2048]{0:T(1024)S(1)}, u32[]{:S(2)}) copy-start(f32[2048]{0:T(1024)S(1)} %get-tuple-element.97) | copy-start | bytes 24580
  95.3 24.9 %copy-start.163 = (f32[2048]{0:T(1024)}, f32[2048]{0:T(1024)S(1)}, u32[]{:S(2)}) copy-start(f32[2048]{0:T(1024)S(1)} %get-tuple-element.98) | copy-start | bytes 24580
  102.7 86.6 %reduce-scatter.19.cloned.1.call-start = ((), (), s32[]{:S(2)}) async-start(), calls=%async_computation.18 | async-start | bytes 2359296 | tf_op jit(solution)/shard_map/reduce_scatter | solution.py:199
  114.4 114.2 %all-gather.7.cloned.1.call-start = ((), (), s32[]{:S(2)}) async-start(), calls=%async_computation.17 | async-start | bytes 4718592 | tf_op jit(solution)/shard_map/all_gather | solution.py:88
  120.3 23.6 %copy-start.67 = (bf16[512,512]{1,0:T(8,128)(2,1)S(1)}, bf16[512,512]{1,0:T(8,128)(2,1)}, u32[]{:S(2)}) copy-start(bf16[512,512]{1,0:T(8,128)(2,1)} %param.31) | copy-start | bytes 1572868
  125.1 21.9 %copy-start.102 = (f32[512]{0:T(512)S(1)}, f32[512]{0:T(512)}, u32[]{:S(2)}) copy-start(f32[512]{0:T(512)} %param.32) | copy-start | bytes 6148
  149.9 110.7 %copy-start.11 = (f32[256,512]{1,0:T(8,128)}, f32[256,512]{1,0:T(8,128)S(1)}, u32[]{:S(2)}) copy-start(f32[256,512]{1,0:T(8,128)S(1)} %get-tuple-element.188) | copy-start | bytes 1572868
  153.2 114.4 %all-gather.9.cloned.1.call-start = ((), (), s32[]{:S(2)}) async-start(), calls=%async_computation.19 | async-start | bytes 4718592 | tf_op jit(solution)/shard_map/all_gather | solution.py:88
  153.8 39.3 %copy-start.168 = (f32[256]{0:T(256)}, f32[256]{0:T(256)S(1)}, u32[]{:S(2)}) copy-start(f32[256]{0:T(256)S(1)} %dynamic-slice_convert_fusion) | copy-start | bytes 3076
  198.5 203.0 %reduce-scatter.25.cloned.1.call-start = ((), (), s32[]{:S(2)}) async-start(), calls=%async_computation.23 | async-start | bytes 4718592 | tf_op jit(solution)/shard_map/reduce_scatter | solution.py:130
  199.5 41.7 %copy-start.72 = (bf16[256,512]{0,1:T(8,128)(2,1)}, bf16[256,512]{0,1:T(8,128)(2,1)S(1)}, u32[]{:S(2)}) copy-start(bf16[256,512]{0,1:T(8,128)(2,1)S(1)} %copy.75) | copy-start | bytes 786436
  261.4 47.9 %copy-start.9 = (f32[256,512]{1,0:T(8,128)}, f32[256,512]{1,0:T(8,128)S(1)}, u32[]{:S(2)}) copy-start(f32[256,512]{1,0:T(8,128)S(1)} %get-tuple-element.192) | copy-start | bytes 1572868
  261.4 47.9 %copy-start.107 = (f32[256]{0:T(256)}, f32[256]{0:T(256)S(1)}, u32[]{:S(2)}) copy-start(f32[256]{0:T(256)S(1)} %broadcast_multiply_fusion.9) | copy-start | bytes 3076
  261.6 47.7 %copy-start.122 = (f32[256]{0:T(256)}, f32[256]{0:T(256)S(1)}, u32[]{:S(2)}) copy-start(f32[256]{0:T(256)S(1)} %fusion.175) | copy-start | bytes 3076
  310.1 21.0 %copy-start.32 = (f32[256,512]{1,0:T(8,128)}, f32[256,512]{1,0:T(8,128)S(1)}, u32[]{:S(2)}) copy-start(f32[256,512]{1,0:T(8,128)S(1)} %get-tuple-element.147) | copy-start | bytes 1572868
  350.1 106.4 %reduce-scatter.21.cloned.1.call-start = ((), (), s32[]{:S(2)}) async-start(), calls=%async_computation.20 | async-start | bytes 4718592 | tf_op jit(solution)/shard_map/reduce_scatter | solution.py:130
  385.6 114.6 %all-gather.11.cloned.1.call-start = ((), (), s32[]{:S(2)}) async-start(), calls=%async_computation.21 | async-start | bytes 2359296 | tf_op jit(solution)/shard_map/all_gather | solution.py:281
  393.4 63.1 %copy-start.91 = (bf16[8,64,256]{2,1,0:T(8,128)(2,1)}, bf16[8,64,256]{2,1,0:T(8,128)(2,1)S(1)}, u32[]{:S(2)}) copy-start(bf16[8,64,256]{2,1,0:T(8,128)(2,1)S(1)} %fusion.90) | copy-start | bytes 786436
  399.5 59.5 %copy-start.89 = (bf16[8,64,256]{2,1,0:T(8,128)(2,1)}, bf16[8,64,256]{2,1,0:T(8,128)(2,1)S(1)}, u32[]{:S(2)}) copy-start(bf16[8,64,256]{2,1,0:T(8,128)(2,1)S(1)} %fusion.91) | copy-start | bytes 786436
  399.5 57.0 %copy-start.12 = (f32[256,512]{1,0:T(8,128)S(1)}, f32[256,512]{1,0:T(8,128)}, u32[]{:S(2)}) copy-start(f32[256,512]{1,0:T(8,128)} %copy-done.11) | copy-start | bytes 1572868
  399.5 57.0 %copy-start.127 = (f32[512]{0:T(512)S(1)}, f32[512]{0:T(512)}, u32[]{:S(2)}) copy-start(f32[512]{0:T(512)} %param.35) | copy-start | bytes 6148
  399.6 57.0 %copy-start.141 = (f32[256]{0:T(256)S(1)}, f32[256]{0:T(256)}, u32[]{:S(2)}) copy-start(f32[256]{0:T(256)} %copy-done.140) | copy-start | bytes 3076
  399.6 57.0 %copy-start.143 = (f32[256]{0:T(256)S(1)}, f32[256]{0:T(256)}, u32[]{:S(2)}) copy-start(f32[256]{0:T(256)} %copy-done.142) | copy-start | bytes 3076
  399.6 57.0 %copy-start.147 = (f32[256]{0:T(256)S(1)}, f32[256]{0:T(256)}, u32[]{:S(2)}) copy-start(f32[256]{0:T(256)} %copy-done.146) | copy-start | bytes 3076
  399.6 57.0 %copy-start.149 = (f32[256]{0:T(256)S(1)}, f32[256]{0:T(256)}, u32[]{:S(2)}) copy-start(f32[256]{0:T(256)} %copy-done.148) | copy-start | bytes 3076
  472.1 28.1 %copy-start.164 = (f32[2048]{0:T(1024)S(1)}, f32[2048]{0:T(1024)}, u32[]{:S(2)}) copy-start(f32[2048]{0:T(1024)} %copy-done.163) | copy-start | bytes 24580
  472.2 57.9 %all-gather.13.cloned.1.call-start = ((), (), s32[]{:S(2)}) async-start(), calls=%async_computation.24 | async-start | bytes 2359296 | tf_op jit(solution)/shard_map/all_gather | solution.py:281
  477.6 145.4 %reduce-scatter.23.cloned.1.call-start = ((), (), s32[]{:S(2)}) async-start(), calls=%async_computation.22 | async-start | bytes 2359296 | tf_op jit(solution)/shard_map/reduce_scatter | solution.py:297
  513.0 111.6 %reduce-scatter.27.cloned.1.call-start = ((), (), s32[]{:S(2)}) async-start(), calls=%async_computation.25 | async-start | bytes 2359296 | tf_op jit(solution)/shard_map/reduce_scatter | solution.py:297
  542.8 115.5 %reduce-scatter.43.cloned.1.call-start = ((), (), s32[]{:S(2)}) async-start(), calls=%async_computation.33 | async-start | bytes 589824 | tf_op jit(solution)/shard_map/reduce_scatter | solution.py:349
  546.1 155.2 %reduce-scatter.45.cloned.1.call-start = ((), (), s32[]{:S(2)}) async-start(), calls=%async_computation.34 | async-start | bytes 2359296 | tf_op jit(solution)/shard_map/reduce_scatter | solution.py:355
  550.7 195.2 %reduce-scatter.47.cloned.1.call-start = ((), (), s32[]{:S(2)}) async-start(), calls=%async_computation.35 | async-start | bytes 2359296 | tf_op jit(solution)/shard_map/reduce_scatter | solution.py:358
  556.4 226.9 %reduce-scatter.35.cloned.1.call-start = ((), (), s32[]{:S(2)}) async-start(), calls=%async_computation.29 | async-start | bytes 589824 | tf_op jit(solution)/shard_map/reduce_scatter | solution.py:331
  559.9 265.1 %reduce-scatter.41.cloned.1.call-start = ((), (), s32[]{:S(2)}) async-start(), calls=%async_computation.32 | async-start | bytes 1769472 | tf_op jit(solution)/shard_map/reduce_scatter | solution.py:346
  563.8 305.6 %reduce-scatter.39.cloned.1.call-start = ((), (), s32[]{:S(2)}) async-start(), calls=%async_computation.31 | async-start | bytes 2359296 | tf_op jit(solution)/shard_map/reduce_scatter | solution.py:340
  572.3 341.8 %reduce-scatter.37.cloned.1.call-start = ((), (), s32[]{:S(2)}) async-start(), calls=%async_computation.30 | async-start | bytes 2359296 | tf_op jit(solution)/shard_map/reduce_scatter | solution.py:337
  584.4 367.3 %reduce-scatter.33.cloned.1.call-start = ((), (), s32[]{:S(2)}) async-start(), calls=%async_computation.28 | async-start | bytes 589824 | tf_op jit(solution)/shard_map/reduce_scatter | solution.py:328
  608.7 381.2 %reduce-scatter.31.cloned.1.call-start = ((), (), s32[]{:S(2)}) async-start(), calls=%async_computation.27 | async-start | bytes 589824 | tf_op jit(solution)/shard_map/reduce_scatter | solution.py:325
  611.6 415.9 %reduce-scatter.29.cloned.1.call-start = ((), (), s32[]{:S(2)}) async-start(), calls=%async_computation.26 | async-start | bytes 589824 | tf_op jit(solution)/shard_map/reduce_scatter | solution.py:322
  626.8 476.8 %all-reduce.14.cloned.1.call-start = ((), (), s32[]{:S(2)}) async-start(), calls=%async_computation.36 | async-start | bytes 3145728 | tf_op jit(solution)/shard_map/psum | solution.py:365
  630.1 398.8 %copy-start.52 = (f32[256,512]{1,0:T(8,128)S(1)}, f32[256,512]{1,0:T(8,128)}, u32[]{:S(2)}) copy-start(f32[256,512]{1,0:T(8,128)} %copy-done.50) | copy-start | bytes 1572868
  (180 other events, 665.9 us)
Sparse Core Ops, SparseCore 0:
  102.9 40.9 reduce-scatter.16
  148.1 41.1 reduce-scatter.18
  191.8 36.7 all-gather.6
  230.9 36.7 all-gather.8
  350.2 51.3 reduce-scatter.24
  405.1 51.3 reduce-scatter.20
  472.3 27.9 all-gather.10
  502.1 27.8 all-gather.12
  533.3 41.2 reduce-scatter.22
  578.1 41.1 reduce-scatter.26
  622.4 34.1 reduce-scatter.42
  660.1 41.2 reduce-scatter.44
  704.7 41.1 reduce-scatter.46
  749.1 34.1 reduce-scatter.34
  786.4 38.4 reduce-scatter.40
  828.1 41.1 reduce-scatter.38
  872.8 41.2 reduce-scatter.36
  917.6 34.1 reduce-scatter.32
  955.7 34.1 reduce-scatter.30
  993.4 34.0 reduce-scatter.28
  1031.0 72.5 all-reduce.13
where the time goes:
time: 1130 us; the launch traced here: 1120 us
  waiting for transfers between devices  594 us (53%)
  matrix products  252 us (22%)
  other arithmetic  88.1 us (8%)
  local copies, waits for them, and re-layouts  85.4 us (8%)
  blocking collectives  81 us (7%)
  between operations  18.5 us (2%)
    psum x1, waiting for transfers between devices, body(): lax.psum(parts[2].astype(jnp.bfloat16), 'grp').astype(jnp.float32)  73.4 us
    dot_general x26, matrix products, product_cols(): lax.dot_general(left, right, (((1,), (1,)), ((), ())), preferred_element_...  64.5 us
    reduce_scatter x2, waiting for transfers between devices, mixer_backward(): lax.psum_scatter(pair_terms.astype(jnp.bfloat16), 'tok', scatter_dimensio...  54.7 us
    unnamed x421, local copies, waits for them, and re-layouts  52.2 us
    dot_general x24, matrix products, product_plain(): return jnp.dot(left, right, preferred_element_type=jnp.float32)  50.7 us
    dot_general x24, matrix products, product_rows(): lax.dot_general(left, right, (((0,), (0,)), ((), ())), preferred_element_...  46.3 us
    reduce_scatter x1, waiting for transfers between devices, body(): lax.psum_scatter(grads['first_up'].astype(jnp.bfloat16), 'tok', scatter_d...  44.8 us
    reduce_scatter x1, waiting for transfers between devices, body(): lax.psum_scatter(grads['second_down'].astype(jnp.bfloat16), 'tok', scatte...  44.5 us
  transfers between devices with their start and end apart: 21, of which 18 were waited for; matrix products, arithmetic and copies ran while one was open for 19% of the time, Pallas kernels for 0%

commit v1 on v0

--- a/solution.py
+++ b/solution.py
@@ -1,6 +1,10 @@
+import functools
+
 import jax
 import jax.numpy as jnp
 from jax import lax
+from jax.experimental import pallas as pl
+from jax.experimental.pallas import tpu as pltpu
 from jax.sharding import PartitionSpec as P
 
 D = 512
@@ -138,7 +142,7 @@
     return (upstream + residual_grad, grad_gain, grad_project, grad_output)
 
 
-def body(
+def general_body(
     tokens,
     latents,
     segments,
@@ -383,52 +387,737 @@
     ) + tuple(summed)
 
 
+TOK = 8
+ROWS = L // TOK
+FF = 2048
+GR = L // LGROUPS
+LOG2E = 1.4426950408889634
+LN2 = 0.6931471805599453
+F32 = jnp.float32
+BF16 = jnp.bfloat16
+MIB = 1024 * 1024
+
+
+def nn(left, right):
+    return lax.dot_general(left, right, (((1,), (0,)), ((), ())), preferred_element_type=F32)
+
+
+def nt(left, right):
+    return lax.dot_general(left, right, (((1,), (1,)), ((), ())), preferred_element_type=F32)
+
+
+def tn(left, right):
+    return lax.dot_general(left, right, (((0,), (0,)), ((), ())), preferred_element_type=F32)
+
+
+def norm_parts(values):
+    centre = values - jnp.mean(values, axis=-1, keepdims=True)
+    inverse = lax.rsqrt(jnp.mean(centre * centre, axis=-1, keepdims=True) + EPS)
+    return centre * inverse, inverse
+
+
+def norm_pull(hat, inverse, gain, upstream):
+    scaled = upstream * gain
+    inner = jnp.mean(scaled * hat, axis=-1, keepdims=True)
+    grad = (scaled - jnp.mean(scaled, axis=-1, keepdims=True) - hat * inner) * inverse
+    return grad, upstream * hat
+
+
+def places():
+    me = lax.axis_index("tok")
+    core = lax.rem(me, 2)
+    chip = lax.div(me, 2)
+    mate = me + 1 - 2 * core
+    flip_x = chip + 1 - 2 * lax.rem(chip, 2)
+    flip_y = lax.rem(chip + 2, 4)
+    far = 3 - chip
+    return me, core, chip, mate, (far, flip_x, flip_y)
+
+
+def remote(src, dst, send_sem, recv_sem, peer):
+    return pltpu.make_async_remote_copy(
+        src_ref=src,
+        dst_ref=dst,
+        send_sem=send_sem,
+        recv_sem=recv_sem,
+        device_id={"tok": peer},
+        device_id_type=pl.DeviceIdType.MESH,
+    )
+
+
+def greet(devices):
+    barrier = pltpu.get_barrier_semaphore()
+    for device in devices:
+        pl.semaphore_signal(
+            barrier, inc=1, device_id={"tok": device}, device_id_type=pl.DeviceIdType.MESH
+        )
+    pl.semaphore_wait(barrier, len(devices))
+
+
+def mask_bias(hot, table):
+    seen = nn(hot, table)
+    bias = (seen - 1.0) * 1e30
+    return jnp.concatenate([bias, bias], axis=1)
+
+
+def cross_forward_kernel(
+    tok_ref, lat_ref, tgain_ref, qgain_ref, qw_ref, kw_ref, vw_ref, hot_ref, tab_ref,
+    k_ref, v_ref, q_ref, acc_ref, ml_ref, vt_ref,
+):
+    @pl.when(pl.program_id(1) == 0)
+    def _():
+        hat, inverse = norm_parts(tok_ref[0, 0].astype(F32))
+        normed = (hat * tgain_ref[...]).astype(BF16)
+        k_ref[0] = nn(normed, kw_ref[...]).astype(BF16)
+        values = nn(normed, vw_ref[...]).astype(BF16)
+        v_ref[0] = values
+        vt_ref[...] = values.T
+
+    hat, inverse = norm_parts(lat_ref[0, 0])
+    normed = (hat * qgain_ref[...]).astype(BF16)
+    queries = (nn(normed, qw_ref[...]) * (D ** (-0.5) * LOG2E)).astype(BF16)
+    q_ref[0] = queries
+    scores = nt(k_ref[0], queries) + mask_bias(hot_ref[0], tab_ref[0, 0])
+    top = jnp.max(scores, axis=0, keepdims=True)
+    raised = jnp.exp2(scores - top)
+    total = jnp.sum(raised, axis=0, keepdims=True)
+    acc_ref[0, 0] = nn(vt_ref[...], raised.astype(BF16)).astype(BF16)
+    ml_ref[0, 0] = jnp.concatenate([top, total, jnp.zeros((6, GR), F32)], axis=0)
+
+
+def cross_forward(tokens, latents, token_gain, query_gain, query_weight, key_weight, value_weight, hot, table):
+    whole = lambda shape: pl.BlockSpec(shape, lambda b, g: (0,) * len(shape))
+    return pl.pallas_call(
+        cross_forward_kernel,
+        grid=(MB, LGROUPS),
+        in_specs=[
+            pl.BlockSpec((1, 1, TOK_DEV, D), lambda b, g: (0, b, 0, 0)),
+            pl.BlockSpec((1, 1, GR, D), lambda b, g: (0, b, g, 0)),
+            whole((1, D)),
+            whole((1, D)),
+            whole((D, D)),
+            whole((D, D)),
+            whole((D, D)),
+            pl.BlockSpec((1, TOK_DEV, 128), lambda b, g: (b, 0, 0)),
+            pl.BlockSpec((1, 1, 128, 128), lambda b, g: (b, g, 0, 0)),
+        ],
+        out_specs=[
+            pl.BlockSpec((1, TOK_DEV, D), lambda b, g: (b, 0, 0)),
+            pl.BlockSpec((1, TOK_DEV, D), lambda b, g: (b, 0, 0)),
+            pl.BlockSpec((1, GR, D), lambda b, g: (b, g, 0)),
+            pl.BlockSpec((1, 1, D, GR), lambda b, g: (g, b, 0, 0)),
+            pl.BlockSpec((1, 1, 8, GR), lambda b, g: (g, b, 0, 0)),
+        ],
+        out_shape=[
+            jax.ShapeDtypeStruct((MB, TOK_DEV, D), BF16),
+            jax.ShapeDtypeStruct((MB, TOK_DEV, D), BF16),
+            jax.ShapeDtypeStruct((MB, L, D), BF16),
+            jax.ShapeDtypeStruct((LGROUPS, MB, D, GR), BF16),
+            jax.ShapeDtypeStruct((LGROUPS, MB, 8, GR), F32),
+        ],
+        scratch_shapes=[pltpu.VMEM((D, TOK_DEV), BF16)],
+        compiler_params=pltpu.CompilerParams(
+            dimension_semantics=("arbitrary", "arbitrary"), vmem_limit_bytes=48 * MIB
+        ),
+        cost_estimate=pl.CostEstimate(
+            flops=14 * 10**9, bytes_accessed=22 * 10**6, transcendentals=4 * 10**6
+        ),
+        name="cross_forward",
+    )(tokens, latents, token_gain, query_gain, query_weight, key_weight, value_weight, hot, table)
+
+
+def gather_sum_kernel(
+    softmax, *refs
+):
+    if softmax:
+        (part_ref, stat_ref, out_ref, lse_ref, mine, got, stage, arrive, total,
+         mine_s, got_s, stage_s, arrive_s, local_sem, core_send, core_recv, chip_send, chip_recv,
+         local_sem_s, core_send_s, core_recv_s, chip_send_s, chip_recv_s) = refs
+    else:
+        (part_ref, out_ref, mine, got, stage, arrive, total,
+         local_sem, core_send, core_recv, chip_send, chip_recv) = refs
+    me, core, chip, mate, others = places()
+    targets = others + (chip,)
+    greet([mate] + [2 * other + core for other in others])
+    locals_, cores = [], []
+    for slot, target in enumerate(targets):
+        own_block = 2 * target + core
+        mate_block = 2 * target + 1 - core
+        cores.append([remote(part_ref.at[mate_block], got.at[slot], core_send.at[slot], core_recv.at[slot], mate)])
+        locals_.append([pltpu.make_async_copy(part_ref.at[own_block], mine.at[slot], local_sem.at[slot])])
+        if softmax:
+            cores[-1].append(remote(stat_ref.at[mate_block], got_s.at[slot], core_send_s.at[slot], core_recv_s.at[slot], mate))
+            locals_[-1].append(pltpu.make_async_copy(stat_ref.at[own_block], mine_s.at[slot], local_sem_s.at[slot]))
+        for copy in cores[-1] + locals_[-1]:
+            copy.start()
+    chips = []
+    for slot, target in enumerate(targets):
+        for copy in locals_[slot]:
+            copy.wait()
+        for copy in cores[slot]:
+            copy.wait_recv()
+        for member in range(MB):
+            left = mine[slot, member].astype(F32)
+            right = got[slot, member].astype(F32)
+            if softmax:
+                left_s, right_s = mine_s[slot, member], got_s[slot, member]
+                top = jnp.maximum(left_s[0:1], right_s[0:1])
+                left_w, right_w = jnp.exp2(left_s[0:1] - top), jnp.exp2(right_s[0:1] - top)
+                added = left * left_w + right * right_w
+                sums = left_s[1:2] * left_w + right_s[1:2] * right_w
+                stage_s[slot, member] = jnp.concatenate([top, sums, jnp.zeros((6, ROWS), F32)], axis=0)
+            else:
+                added = left + right
+            if slot == 3:
+                total[member] = added
+            else:
+                stage[slot, member] = added.astype(BF16)
+        if slot < 3:
+            peer = 2 * target + core
+            chips.append([remote(stage.at[slot], arrive.at[slot], chip_send.at[slot], chip_recv.at[slot], peer)])
+            if softmax:
+                chips[-1].append(remote(stage_s.at[slot], arrive_s.at[slot], chip_send_s.at[slot], chip_recv_s.at[slot], peer))
+            for copy in chips[-1]:
+                copy.start()
+    for slot in (1, 2, 0):
+        for copy in chips[slot]:
+            copy.wait_recv()
+        for member in range(MB):
+            new = arrive[slot, member].astype(F32)
+            if softmax:
+                left_s, right_s = stage_s[3, member], arrive_s[slot, member]
+                top = jnp.maximum(left_s[0:1], right_s[0:1])
+                left_w, right_w = jnp.exp2(left_s[0:1] - top), jnp.exp2(right_s[0:1] - top)
+                total[member] = total[member] * left_w + new * right_w
+                sums = left_s[1:2] * left_w + right_s[1:2] * right_w
+                stage_s[3, member] = jnp.concatenate([top, sums, jnp.zeros((6, ROWS), F32)], axis=0)
+            else:
+                total[member] = total[member] + new
+    for member in range(MB):
+        if softmax:
+            stats = stage_s[3, member]
+            out_ref[member] = (total[member] / stats[1:2]).T
+            lse = stats[0:1] + jnp.log2(stats[1:2])
+            lse_ref[member] = jnp.concatenate([lse, jnp.zeros((7, ROWS), F32)], axis=0)
+        else:
+            out_ref[member] = total[member].T
+    for group in cores + chips:
+        for copy in group:
+            copy.wait_send()
+
+
+def gather_sum(softmax, collective_id, *parts):
+    dma = pltpu.SemaphoreType.DMA
+    data = [
+        pltpu.VMEM((4, MB, D, ROWS), BF16),
+        pltpu.VMEM((4, MB, D, ROWS), BF16),
+        pltpu.VMEM((3, MB, D, ROWS), BF16),
+        pltpu.VMEM((3, MB, D, ROWS), BF16),
+        pltpu.VMEM((MB, D, ROWS), F32),
+    ]
+    sems = [dma((4,)), dma((4,)), dma((4,)), dma((3,)), dma((3,))]
+    out_shape = [jax.ShapeDtypeStruct((MB, ROWS, D), F32)]
+    scratch = data + sems
+    if softmax:
+        stats = [
+            pltpu.VMEM((4, MB, 8, ROWS), F32),
+            pltpu.VMEM((4, MB, 8, ROWS), F32),
+            pltpu.VMEM((4, MB, 8, ROWS), F32),
+            pltpu.VMEM((3, MB, 8, ROWS), F32),
+        ]
+        scratch = data + stats + sems + [dma((4,)), dma((4,)), dma((4,)), dma((3,)), dma((3,))]
+        out_shape.append(jax.ShapeDtypeStruct((MB, 8, ROWS), F32))
+    return pl.pallas_call(
+        functools.partial(gather_sum_kernel, softmax),
+        in_specs=[pl.BlockSpec(memory_space=pl.ANY)] * len(parts),
+        out_specs=[pl.BlockSpec(memory_space=pltpu.VMEM)] * len(out_shape),
+        out_shape=out_shape,
+        scratch_shapes=scratch,
+        compiler_params=pltpu.CompilerParams(
+            collective_id=collective_id, has_side_effects=True, vmem_limit_bytes=48 * MIB
+        ),
+        name="weighted_sum" if softmax else "query_grad_sum",
+    )(*parts)
+
+
+def exchange_kernel(to_heads, src_ref, dst_ref, send_sem, recv_sem, local_sem):
+    me, core, chip, mate, others = places()
+    peers = []
+    for other in others:
+        peers += [2 * other + core, 2 * other + 1 - core]
+    peers.append(mate)
+    greet(peers)
+
+    def ends(mine, device, member):
+        rows_lane = pl.ds(member * ROWS, ROWS)
+        if to_heads:
+            source = src_ref.at[:, device, :, rows_lane]
+            target = dst_ref.at[:, member, :, pl.ds(pl.multiple_of(mine * ROWS, ROWS), ROWS)]
+        else:
+            source = src_ref.at[:, member, :, pl.ds(pl.multiple_of(device * ROWS, ROWS), ROWS)]
+            target = dst_ref.at[:, mine, :, rows_lane]
+        return source, target
+
+    copies = []
+    for slot, peer in enumerate(peers):
+        for member in range(MB):
+            source, target = ends(me, peer, member)
+            copies.append(remote(source, target, send_sem.at[slot, member], recv_sem.at[slot, member], peer))
+            copies[-1].start()
+    own = []
+    for member in range(MB):
+        source, target = ends(me, me, member)
+        own.append(pltpu.make_async_copy(source, target, local_sem.at[member]))
+        own[-1].start()
+    for copy in own:
+        copy.wait()
+    for copy in copies:
+        copy.wait()
+
+
+def exchange(to_heads, collective_id, source):
+    kinds = source.shape[0]
+    shape = (kinds, MB, HD, L) if to_heads else (kinds, H, HD, MB * ROWS)
+    dma = pltpu.SemaphoreType.DMA
+    return pl.pallas_call(
+        functools.partial(exchange_kernel, to_heads),
+        in_specs=[pl.BlockSpec(memory_space=pl.ANY)],
+        out_specs=pl.BlockSpec(memory_space=pl.ANY),
+        out_shape=jax.ShapeDtypeStruct(shape, source.dtype),
+        scratch_shapes=[dma((7, MB)), dma((7, MB)), dma((MB,))],
+        compiler_params=pltpu.CompilerParams(collective_id=collective_id, has_side_effects=True),
+        name="exchange",
+    )(source)
+
+
+def share_kernel(data_ref, stat_ref, all_ref, stats_ref, near_send, near_recv, far_send, far_recv, on_send, on_recv, local_sem):
+    me, core, chip, mate, others = places()
+    greet([mate] + [2 * other + core for other in others])
+    pairs = ((data_ref, all_ref), (stat_ref, stats_ref))
+    local, near, far, on = [], [], [], []
+    for slot, other in enumerate(others):
+        for kind, (source, target) in enumerate(pairs):
+            far.append(remote(source, target.at[me], far_send.at[slot, kind], far_recv.at[slot, kind], 2 * other + core))
+            far[-1].start()
+    for kind, (source, target) in enumerate(pairs):
+        near.append(remote(source, target.at[me], near_send.at[kind], near_recv.at[kind], mate))
+        near[-1].start()
+        local.append(pltpu.make_async_copy(source, target.at[me], local_sem.at[kind]))
+        local[-1].start()
+    for slot in (1, 2, 0):
+        for kind, (source, target) in enumerate(pairs):
+            far[2 * slot + kind].wait_recv()
+            place = target.at[2 * others[slot] + core]
+            on.append(remote(place, place, on_send.at[slot, kind], on_recv.at[slot, kind], mate))
+            on[-1].start()
+    for copy in local + near + on:
+        copy.wait()
+    for copy in far:
+        copy.wait_send()
+
+
+def share(collective_id, data, stats):
+    dma = pltpu.SemaphoreType.DMA
+    return pl.pallas_call(
+        share_kernel,
+        in_specs=[pl.BlockSpec(memory_space=pl.ANY)] * 2,
+        out_specs=[pl.BlockSpec(memory_space=pl.ANY)] * 2,
+        out_shape=[
+            jax.ShapeDtypeStruct((TOK,) + data.shape, data.dtype),
+            jax.ShapeDtypeStruct((TOK,) + stats.shape, stats.dtype),
+        ],
+        scratch_shapes=[dma((2,)), dma((2,)), dma((3, 2)), dma((3, 2)), dma((3, 2)), dma((3, 2)), dma((2,))],
+        compiler_params=pltpu.CompilerParams(collective_id=collective_id, has_side_effects=True),
+        name="share_grads",
+    )(data, stats)
+
+
+def mixer_attend_kernel(all_ref, q_ref, mixed_ref, exact_ref, lse_ref, keys, values):
+    @pl.when(pl.program_id(1) == 0)
+    def _():
+        keys[...] = all_ref[1, 0].T
+        values[0:HD] = all_ref[2, 0]
+        values[HD:] = jnp.ones((16, L), BF16)
+
+    logits = nn(keys[...], q_ref[0, 0])
+    top = jnp.max(logits, axis=0, keepdims=True)
+    raised = jnp.exp2(logits - top).astype(BF16)
+    both = nn(values[...], raised)
+    total = both[HD:HD + 1]
+    mixed = both[0:HD] / total
+    exact_ref[0] = mixed
+    mixed_ref[0, 0] = mixed.astype(BF16)
+    lse = top + jnp.log2(total)
+    lse_ref[0] = jnp.concatenate([lse, jnp.zeros((7, lse.shape[1]), F32)], axis=0)
+
+
+QB = 256
+
+
+def mixer_attend(packed):
+    return pl.pallas_call(
+        mixer_attend_kernel,
+        grid=(MB, L // QB),
+        in_specs=[
+            pl.BlockSpec((3, 1, HD, L), lambda b, i: (0, b, 0, 0)),
+            pl.BlockSpec((1, 1, HD, QB), lambda b, i: (0, b, 0, i)),
+        ],
+        out_specs=[
+            pl.BlockSpec((1, 1, HD, QB), lambda b, i: (0, b, 0, i)),
+            pl.BlockSpec((1, HD, QB), lambda b, i: (b, 0, i)),
+            pl.BlockSpec((1, 8, QB), lambda b, i: (b, 0, i)),
+        ],
+        out_shape=[
+            jax.ShapeDtypeStruct((1, MB, HD, L), BF16),
+            jax.ShapeDtypeStruct((MB, HD, L), F32),
+            jax.ShapeDtypeStruct((MB, 8, L), F32),
+        ],
+        scratch_shapes=[pltpu.VMEM((L, HD), BF16), pltpu.VMEM((HD + 16, L), BF16)],
+        compiler_params=pltpu.CompilerParams(
+            dimension_semantics=("arbitrary", "arbitrary"), vmem_limit_bytes=48 * MIB
+        ),
+        cost_estimate=pl.CostEstimate(
+            flops=9 * 10**9, bytes_accessed=4 * 10**6, transcendentals=8 * 10**6
+        ),
+        name="mixer_attend",
+    )(packed, packed)
+
+
+def mixer_attend_back_kernel(all_ref, q_ref, up_ref, exact_ref, lse_ref, out_ref, keys, values, key_acc, value_acc):
+    step = pl.program_id(1)
+
+    @pl.when(step == 0)
+    def _():
+        keys[...] = all_ref[1, 0].T
+        values[...] = all_ref[2, 0].T
+        key_acc[...] = jnp.zeros_like(key_acc)
+        value_acc[...] = jnp.zeros_like(value_acc)
+
+    queries = q_ref[0, 0]
+    upstream = up_ref[0, 0]
+    inner = jnp.sum(upstream.astype(F32) * exact_ref[0], axis=0, keepdims=True)
+    softened = jnp.exp2(nn(keys[...], queries) - lse_ref[0][0:1])
+    soft_grad = nn(values[...], upstream)
+    logit_grad = (softened * (soft_grad - inner)).astype(BF16)
+    value_acc[...] += nt(upstream, softened.astype(BF16))
+    key_acc[...] += nt(queries, logit_grad)
+    query_grad = nn(all_ref[1, 0], logit_grad) * HD ** (-0.5)
+    out_ref[0, 0, :, pl.ds(pl.multiple_of(step * QB, QB), QB)] = query_grad.astype(BF16)
+
+    @pl.when(step == L // QB - 1)
+    def _():
+        out_ref[1, 0] = (key_acc[...] * LN2).astype(BF16)
+        out_ref[2, 0] = value_acc[...].astype(BF16)
+
+
+def mixer_attend_back(packed, upstream, exact, lse):
+    return pl.pallas_call(
+        mixer_attend_back_kernel,
+        grid=(MB, L // QB),
+        in_specs=[
+            pl.BlockSpec((3, 1, HD, L), lambda b, i: (0, b, 0, 0)),
+            pl.BlockSpec((1, 1, HD, QB), lambda b, i: (0, b, 0, i)),
+            pl.BlockSpec((1, 1, HD, QB), lambda b, i: (0, b, 0, i)),
+            pl.BlockSpec((1, HD, QB), lambda b, i: (b, 0, i)),
+            pl.BlockSpec((1, 8, QB), lambda b, i: (b, 0, i)),
+        ],
+        out_specs=pl.BlockSpec((3, 1, HD, L), lambda b, i: (0, b, 0, 0)),
+        out_shape=jax.ShapeDtypeStruct((3, MB, HD, L), BF16),
+        scratch_shapes=[
+            pltpu.VMEM((L, HD), BF16),
+            pltpu.VMEM((L, HD), BF16),
+            pltpu.VMEM((HD, L), F32),
+            pltpu.VMEM((HD, L), F32),
+        ],
+        compiler_params=pltpu.CompilerParams(
+            dimension_semantics=("arbitrary", "arbitrary"), vmem_limit_bytes=48 * MIB
+        ),
+        cost_estimate=pl.CostEstimate(
+            flops=22 * 10**9, bytes_accessed=5 * 10**6, transcendentals=8 * 10**6
+        ),
+        name="mixer_attend_back",
+    )(packed, packed, upstream, exact, lse)
+
+
+def cross_backward_kernel(
+    tok_ref, tgain_ref, kw_ref, vw_ref, hot_ref, tab_ref, k_ref, v_ref, q_ref, up_ref, stat_ref,
+    dq_ref, dtok_ref, dkw_ref, dvw_ref, dgain_ref, kt_ref, dk_ref, dv_ref,
+):
+    member, step = pl.program_id(0), pl.program_id(1)
+
+    @pl.when(step == 0)
+    def _():
+        kt_ref[...] = k_ref[0].T
+        dk_ref[...] = jnp.zeros_like(dk_ref)
+        dv_ref[...] = jnp.zeros_like(dv_ref)
+
+    queries = q_ref[0]
+    upstream = up_ref[0, 0]
+    stats = stat_ref[0, 0]
+    scores = nt(k_ref[0], queries) + mask_bias(hot_ref[0], tab_ref[0, 0])
+    weights = jnp.exp2(scores - stats[0:1])
+    dv_ref[...] += nn(weights.astype(BF16), upstream)
+    score_grad = (weights * (nt(v_ref[0], upstream) - stats[1:2])).astype(BF16)
+    dk_ref[...] += nn(score_grad, queries)
+    dq_ref[0, 0] = (nn(kt_ref[...], score_grad) * D ** (-0.5)).astype(BF16)
+
+    @pl.when(step == LGROUPS - 1)
+    def _():
+        gain = tgain_ref[...]
+        hat, inverse = norm_parts(tok_ref[0, 0].astype(F32))
+        normed = (hat * gain).astype(BF16)
+        key_grad = (dk_ref[...] * LN2).astype(BF16)
+        value_grad = dv_ref[...].astype(BF16)
+        key_term = tn(normed, key_grad)
+        value_term = tn(normed, value_grad)
+        normed_grad = nt(key_grad, kw_ref[...]) + nt(value_grad, vw_ref[...])
+        source_grad, gain_rows = norm_pull(hat, inverse, gain, normed_grad)
+        dtok_ref[0, 0] = source_grad
+        gain_term = jnp.sum(gain_rows, axis=0, keepdims=True)
+
+        @pl.when(member == 0)
+        def _():
+            dkw_ref[...] = key_term
+            dvw_ref[...] = value_term
+            dgain_ref[...] = gain_term
+
+        @pl.when(member > 0)
+        def _():
+            dkw_ref[...] += key_term
+            dvw_ref[...] += value_term
+            dgain_ref[...] += gain_term
+
+
+def cross_backward(tokens, token_gain, key_weight, value_weight, hot, table, keys, values, queries, upstream, stats):
+    whole = lambda shape: pl.BlockSpec(shape, lambda b, g: (0,) * len(shape))
+    return pl.pallas_call(
+        cross_backward_kernel,
+        grid=(MB, LGROUPS),
+        in_specs=[
+            pl.BlockSpec((1, 1, TOK_DEV, D), lambda b, g: (0, b, 0, 0)),
+            whole((1, D)),
+            whole((D, D)),
+            whole((D, D)),
+            pl.BlockSpec((1, TOK_DEV, 128), lambda b, g: (b, 0, 0)),
+            pl.BlockSpec((1, 1, 128, 128), lambda b, g: (b, g, 0, 0)),
+            pl.BlockSpec((1, TOK_DEV, D), lambda b, g: (b, 0, 0)),
+            pl.BlockSpec((1, TOK_DEV, D), lambda b, g: (b, 0, 0)),
+            pl.BlockSpec((1, GR, D), lambda b, g: (b, g, 0)),
+            pl.BlockSpec((1, 1, GR, D), lambda b, g: (g, b, 0, 0)),
+            pl.BlockSpec((1, 1, 8, GR), lambda b, g: (g, b, 0, 0)),
+        ],
+        out_specs=[
+            pl.BlockSpec((1, 1, D, GR), lambda b, g: (g, b, 0, 0)),
+            pl.BlockSpec((1, 1, TOK_DEV, D), lambda b, g: (0, b, 0, 0)),
+            whole((D, D)),
+            whole((D, D)),
+            whole((1, D)),
+        ],
+        out_shape=[
+            jax.ShapeDtypeStruct((LGROUPS, MB, D, GR), BF16),
+            jax.ShapeDtypeStruct((1, MB, TOK_DEV, D), F32),
+            jax.ShapeDtypeStruct((D, D), F32),
+            jax.ShapeDtypeStruct((D, D), F32),
+            jax.ShapeDtypeStruct((1, D), F32),
+        ],
+        scratch_shapes=[
+            pltpu.VMEM((D, TOK_DEV), BF16),
+            pltpu.VMEM((TOK_DEV, D), F32),
+            pltpu.VMEM((TOK_DEV, D), F32),
+        ],
+        compiler_params=pltpu.CompilerParams(
+            dimension_semantics=("arbitrary", "arbitrary"), vmem_limit_bytes=56 * MIB
+        ),
+        cost_estimate=pl.CostEstimate(
+            flops=26 * 10**9, bytes_accessed=24 * 10**6, transcendentals=4 * 10**6
+        ),
+        name="cross_backward",
+    )(tokens, token_gain, key_weight, value_weight, hot, table, keys, values, queries, upstream, stats)
+
+
+def reduce_grads(columns, rows):
+    part = lax.psum_scatter(columns.astype(BF16), "tok", scatter_dimension=0, tiled=True)
+    other = lax.psum_scatter(rows.astype(BF16), "tok", scatter_dimension=0, tiled=True)
+    return lax.psum((part, other), "grp")
+
+
+def fast_body(
+    tokens,
+    latents,
+    segments,
+    scene_mask,
+    counts,
+    token_gain,
+    query_gain,
+    query_weight,
+    key_weight,
+    value_weight,
+    output_weight,
+    first_gain,
+    first_up,
+    first_down,
+    mixer_gain,
+    mixer_project,
+    mixer_output,
+    second_gain,
+    second_up,
+    second_down,
+    cotangent,
+):
+    me = lax.axis_index("tok")
+    lanes = jnp.arange(128)
+    alive = jnp.arange(TOK_DEV)[None, :] < counts[0]
+    hot = (segments[0][:, :, None] == lanes[None, None, :]) & alive[:, :, None]
+    hot = hot.astype(BF16)
+    table = jnp.pad(scene_mask[0].transpose(0, 2, 1), ((0, 0), (0, 0), (0, 128 - SCENES)))
+    table = jnp.broadcast_to((table > 0)[..., None], (MB, LGROUPS, 128, 128)).astype(BF16)
+
+    keys, values, queries, weighted, figures = cross_forward(
+        tokens, latents, token_gain[None], query_gain[None], query_weight, key_weight, value_weight, hot, table
+    )
+    attended, lse = gather_sum(True, 0, weighted, figures)
+    attended = attended.reshape(MB * ROWS, D)
+    latent_in = lax.dynamic_slice_in_dim(latents[0], me * ROWS, ROWS, 1).reshape(MB * ROWS, D)
+
+    attended_low = attended.astype(BF16)
+    first_mid = latent_in + nn(attended_low, output_weight)
+    mixer_mid, first_saved = mlp_forward(first_mid, first_gain, first_up, first_down)
+
+    mixer_normed = norm_rows(mixer_mid, mixer_gain).astype(BF16)
+    packed = lax.dot_general(
+        mixer_project, mixer_normed, (((0,), (1,)), ((), ())), preferred_element_type=F32
+    ).reshape(3, D, MB * ROWS)
+    packed = packed * jnp.array([HD ** (-0.5) * LOG2E, 1.0, 1.0], F32)[:, None, None]
+    packed = packed.astype(BF16).reshape(3, H, HD, MB * ROWS)
+    head_packed = exchange(True, 1, packed)
+    head_mixed, head_exact, head_lse = mixer_attend(head_packed)
+    mixed = exchange(False, 2, head_mixed).reshape(D, MB * ROWS)
+    second_mid = mixer_mid + tn(mixed, mixer_output)
+    final_rows, second_saved = mlp_forward(second_mid, second_gain, second_up, second_down)
+
+    upstream = cotangent.reshape(MB * ROWS, D)
+    upstream, d_second_gain, d_second_up, d_second_down = mlp_backward(
+        second_mid, second_gain, second_up, second_down, second_saved, upstream
+    )
+    grad_low = upstream.astype(BF16)
+    d_mixer_output = nn(mixed, grad_low)
+    mixed_grad = nt(mixer_output, grad_low).astype(BF16).reshape(1, H, HD, MB * ROWS)
+    head_grad = mixer_attend_back(head_packed, exchange(True, 3, mixed_grad), head_exact, head_lse)
+    packed_grad = exchange(False, 4, head_grad).reshape(3 * D, MB * ROWS)
+    d_mixer_project = lax.dot_general(
+        mixer_normed, packed_grad, (((0,), (1,)), ((), ())), preferred_element_type=F32
+    )
+    normed_grad = lax.dot_general(
+        packed_grad, mixer_project, (((0,), (1,)), ((), ())), preferred_element_type=F32
+    )
+    residual_grad, d_mixer_gain = norm_back(mixer_mid, mixer_gain, normed_grad)
+    upstream, d_first_gain, d_first_up, d_first_down = mlp_backward(
+        first_mid, first_gain, first_up, first_down, first_saved, upstream + residual_grad
+    )
+    grad_low = upstream.astype(BF16)
+    d_output = tn(attended_low, grad_low)
+    attended_grad = nt(grad_low, output_weight).astype(BF16)
+    inner = jnp.sum(attended_grad.astype(F32) * attended, axis=1).reshape(MB, ROWS)
+    figures = jnp.concatenate(
+        [lse[:, 0:1], inner[:, None], jnp.zeros((MB, 6, ROWS), F32)], axis=1
+    )
+    upstream_all, figures_all = share(5, attended_grad.reshape(MB, ROWS, D), figures)
+    query_part, tokens_grad, d_key, d_value, d_token_gain = cross_backward(
+        tokens, token_gain[None], key_weight, value_weight, hot, table, keys, values, queries,
+        upstream_all, figures_all,
+    )
+    query_grad = gather_sum(False, 6, query_part)[0].reshape(MB * ROWS, D).astype(BF16)
+    latent_normed = norm_rows(latent_in, query_gain).astype(BF16)
+    d_query = tn(latent_normed, query_grad)
+    latent_grad, d_query_gain = norm_back(latent_in, query_gain, nt(query_grad, query_weight))
+    latent_grad = upstream + latent_grad
+
+    columns, rows = reduce_grads(
+        jnp.concatenate(
+            [d_second_up, d_mixer_output, d_mixer_project, d_first_up, d_output, d_key, d_value, d_query,
+             jnp.pad(jnp.stack([d_second_gain, d_mixer_gain, d_first_gain, d_token_gain[0], d_query_gain], axis=1), ((0, 0), (0, 123)))], axis=1
+        ),
+        jnp.concatenate([d_second_down, d_first_down], axis=1),
+    )
+    columns = columns.astype(F32)
+    rows = rows.astype(F32)
+    widths = [FF, D, 3 * D, FF, D, D, D, D, 128]
+    cuts = [sum(widths[:i]) for i in range(len(widths) + 1)]
+    (o_second_up, o_mixer_output, o_mixer_project, o_first_up, o_output, o_key, o_value, o_query, o_gains) = [
+        columns[:, cuts[i]:cuts[i + 1]] for i in range(len(widths))
+    ]
+    return (
+        final_rows.reshape(1, MB, ROWS, D),
+        latent_grad.reshape(1, MB, ROWS, D),
+        tokens_grad,
+        o_gains[:, 3],
+        o_gains[:, 4],
+        o_query,
+        o_key,
+        o_value,
+        o_output,
+        o_gains[:, 2],
+        o_first_up,
+        rows[:, D:],
+        o_gains[:, 1],
+        o_mixer_project,
+        o_mixer_output,
+        o_gains[:, 0],
+        o_second_up,
+        rows[:, :D],
+    )
+
+
+IN_SPECS = (
+    P("grp", None, "tok", None),
+    P("grp", None, None, None),
+    P("grp", None, "tok"),
+    P("grp", None, None, None),
+    P("grp", None, "tok"),
+    P(),
+    P(),
+    P(),
+    P(),
+    P(),
+    P(),
+    P(),
+    P(),
+    P(),
+    P(),
+    P(),
+    P(),
+    P(),
+    P(),
+    P(),
+    P("grp", None, "tok", None),
+)
+OUT_SPECS = (
+    P("grp", None, "tok", None),
+    P("grp", None, "tok", None),
+    P("grp", None, "tok", None),
+    P("tok"),
+    P("tok"),
+    P("tok", None),
+    P("tok", None),
+    P("tok", None),
+    P("tok", None),
+    P("tok"),
+    P("tok", None),
+    P("tok", None),
+    P("tok"),
+    P("tok", None),
+    P("tok", None),
+    P("tok"),
+    P("tok", None),
+    P("tok", None),
+)
+
+
 def solution(mesh):
     return jax.shard_map(
-        body,
+        fast_body if mesh.shape["tok"] == TOK else general_body,
         mesh=mesh,
-        in_specs=(
-            P("grp", None, "tok", None),
-            P("grp", None, None, None),
-            P("grp", None, "tok"),
-            P("grp", None, None, None),
-            P("grp", None, "tok"),
-            P(),
-            P(),
-            P(),
-            P(),
-            P(),
-            P(),
-            P(),
-            P(),
-            P(),
-            P(),
-            P(),
-            P(),
-            P(),
-            P(),
-            P(),
-            P("grp", None, "tok", None),
-        ),
-        out_specs=(
-            P("grp", None, "tok", None),
-            P("grp", None, "tok", None),
-            P("grp", None, "tok", None),
-            P("tok"),
-            P("tok"),
-            P("tok", None),
-            P("tok", None),
-            P("tok", None),
-            P("tok", None),
-            P("tok"),
-            P("tok", None),
-            P("tok", None),
-            P("tok"),
-            P("tok", None),
-            P("tok", None),
-            P("tok"),
-            P("tok", None),
-            P("tok", None),
-        ),
+        in_specs=IN_SPECS,
+        out_specs=OUT_SPECS,
         check_vma=False,
     )

time: 1130 us -> 564 us (0.50)
  waiting for transfers between devices: 594 us -> 140 us
  Pallas kernels: 0 us -> 291 us
  matrix products: 252 us -> 52.2 us
  blocking collectives: 81 us -> 0 us
  other arithmetic: 88.1 us -> 23 us
  local copies, waits for them, and re-layouts: 85.4 us -> 33.5 us
    reduce_scatter x16 -> x2, waiting for transfers between devices: 466 us -> 72.6 us  [the longest x1 72.6 us: reduce_grads(): lax.psum_scatter(columns.astype(BF16), 'tok', scatter_dimension=0, tiled=...]
    pallas_call x0 -> x11, Pallas kernels: none -> 291 us  [the longest x4 61.3 us: exchange(): pl.pallas_call(functools.partial(exchange_kernel, to_heads), in_specs=[pl...]
    all_gather x4 -> x0, waiting for transfers between devices: 54.6 us -> none  [the longest x2 34.2 us: mixer_forward(): pair_rows = lax.all_gather(packed[:, D:], 'tok', axis=0, tiled=True)]
    dot_general x26 -> x4, matrix products: 64.5 us -> 10.8 us  [product_cols(): lax.dot_general(left, right, (((1,), (1,)), ((), ())), preferred_element_...]
    dot_general x10 -> x11, matrix products: 70.7 us -> 19.6 us  [the longest x3 4.89 us: tn(): lax.dot_general(left, right, (((0,), (0,)), ((), ())), preferred_element_...]
    dot_general x24 -> x4, matrix products: 50.7 us -> 9.05 us  [product_plain(): return jnp.dot(left, right, preferred_element_type=jnp.float32)]
    dot_general x24 -> x4, matrix products: 46.3 us -> 12.7 us  [product_rows(): lax.dot_general(left, right, (((0,), (0,)), ((), ())), preferred_element_...]
    unnamed x421 -> x146, local copies, waits for them, and re-layouts: 52.2 us -> 20 us
  transfers between devices with their start and end apart: 21 -> 3, of which waited for: 18 -> 2; matrix products, arithmetic and copies ran while one was open for 19% -> 6% of each run, Pallas kernels for 0% -> 21%
where the time goes in v1:
time: 564 us; the launch traced here: 555 us
  Pallas kernels  291 us (52%)
  waiting for transfers between devices  140 us (25%)
  matrix products  52.2 us (9%)
  local copies, waits for them, and re-layouts  33.5 us (6%)
  other arithmetic  23 us (4%)
  between operations  14.9 us (3%)
    reduce_scatter x1, waiting for transfers between devices, reduce_grads(): lax.psum_scatter(columns.astype(BF16), 'tok', scatter_dimension=0, tiled=...  72.6 us
    psum x1, waiting for transfers between devices, reduce_grads(): return lax.psum((part, other), 'grp')  67.3 us
    pallas_call x4, Pallas kernels, exchange(): pl.pallas_call(functools.partial(exchange_kernel, to_heads), in_specs=[pl...  61.3 us
    pallas_call x2, Pallas kernels, gather_sum(): pl.pallas_call(functools.partial(gather_sum_kernel, softmax), in_specs=[p...  60.5 us
    pallas_call x1, Pallas kernels, cross_backward(): pl.pallas_call(cross_backward_kernel, grid=(MB, LGROUPS), in_specs=[pl.Bl...  45.4 us
    pallas_call x1, Pallas kernels, share(): pl.pallas_call(share_kernel, in_specs=[pl.BlockSpec(memory_space=pl.ANY)]...  41.4 us
    pallas_call x1, Pallas kernels, cross_forward(): pl.pallas_call(cross_forward_kernel, grid=(MB, LGROUPS), in_specs=[pl.Blo...  36.8 us
    pallas_call x1, Pallas kernels, mixer_attend_back(): pl.pallas_call(mixer_attend_back_kernel, grid=(MB, L // QB), in_specs=[pl...  24.9 us
  transfers between devices with their start and end apart: 3, of which 2 were waited for; matrix products, arithmetic and copies ran while one was open for 6% of the time, Pallas kernels for 21%

profile of v1, /device:TPU:0, one launch (start us, length us, event | category | flops | bytes accessed | tf_op | source)
XLA Modules:
  0.0 554.6 jit_solution(18163313235057493379)
XLA Ops:
  9.0 2.1 bitcast_convert_fusion
  11.1 1.9 fusion.22.hot_ref
  13.0 1.6 fusion.42
  16.0 36.8 %cross_forward.1 = (bf16[2,1024,512]{2,1,0:T(8,128)(2,1)S(1)}, bf16[2,1024,512]{2,1,0:T(8,128)(2,1)}, bf16[2,2048,512]{2,1,0:T(8,128)(2,1)}, bf16[8,2,512,256]{3,2,1,0:T(8,128)(2,1)}, f32[8,2,8,256]{3,2,1,0:T(8,128)S(1)}) custom-call(bf16[1,2,1024,512]{3,2,1,0:T(8,128)(2,1)} %tok_ref.3, f32[1,2,2048,512]{3,2,1,0:T(8,128)} %lat_ref.1, f32[1,512]{1,0:T(1,128)S(1)} %bitcast.77, ...), custom_call_target="tpu_custom_call" | custom-call | flops 14000000000 | bytes 22000000 | tf_op jit(solution)/shard_map/cross_forward/pallas_call | solution.py:490
  52.9 1.4 copy-done.17
  54.3 2.2 copy-done.3
  56.5 31.5 %weighted_sum.1 = (f32[2,256,512]{2,1,0:T(8,128)S(1)}, f32[2,8,256]{2,1,0:T(8,128)S(1)}) custom-call(bf16[8,2,512,256]{3,2,1,0:T(8,128)(2,1)S(1)} %copy-done.3, f32[8,2,8,256]{3,2,1,0:T(8,128)S(1)} %get-tuple-element.36.refs_1_), custom_call_target="tpu_custom_call" | custom-call | tf_op jit(solution)/shard_map/weighted_sum/pallas_call | solution.py:630
  88.9 1.3 fusion.39
  90.6 1.6 fusion.50
  93.6 2.8 convolution_bitcast_fusion
  96.4 3.6 copy.68
  100.0 3.6 multiply_convert_fusion.2.src_ref
  103.6 20.9 %exchange.4.all_ref.q_ref = bf16[3,2,64,2048]{3,2,1,0:T(8,128)(2,1)} custom-call(bf16[3,8,64,512]{3,2,1,0:T(8,128)(2,1)} %multiply_convert_fusion.2.src_ref), custom_call_target="tpu_custom_call" | custom-call | tf_op jit(solution)/shard_map/exchange/pallas_call | solution.py:682
  124.5 1.4 copy-done.4
  125.9 20.5 %mixer_attend.1 = (bf16[1,2,64,2048]{3,2,1,0:T(8,128)(2,1)S(1)}, f32[2,64,2048]{2,1,0:T(8,128)S(1)}, f32[2,8,2048]{2,1,0:T(8,128)S(1)}) custom-call(bf16[3,2,64,2048]{3,2,1,0:T(8,128)(2,1)S(1)} %copy-done.4, bf16[3,2,64,2048]{3,2,1,0:T(8,128)(2,1)S(1)} %copy-done.4), custom_call_target="tpu_custom_call" | custom-call | flops 8999999488 | bytes 4000000 | tf_op jit(solution)/shard_map/mixer_attend/pallas_call | solution.py:758
  148.2 9.9 %exchange.5 = bf16[1,8,64,512]{3,2,1,0:T(8,128)(2,1)} custom-call(bf16[1,2,64,2048]{3,2,1,0:T(8,128)(2,1)} %copy-done.10), custom_call_target="tpu_custom_call" | custom-call | tf_op jit(solution)/shard_map/exchange/pallas_call | solution.py:682
  158.1 2.2 fusion.51
  160.7 1.3 fusion.52
  162.0 3.7 fusion.13
  165.8 3.4 convolution_convert_fusion.2
  169.2 1.5 multiply_reduce_fusion.3
  173.7 9.2 %exchange.6.up_ref = bf16[1,2,64,2048]{3,2,1,0:T(8,128)(2,1)} custom-call(bf16[1,8,64,512]{3,2,1,0:T(8,128)(2,1)} %bitcast.85), custom_call_target="tpu_custom_call" | custom-call | tf_op jit(solution)/shard_map/exchange/pallas_call | solution.py:682
  185.2 24.9 %mixer_attend_back.1.src_ref = bf16[3,2,64,2048]{3,2,1,0:T(8,128)(2,1)S(1)} custom-call(bf16[3,2,64,2048]{3,2,1,0:T(8,128)(2,1)S(1)} %copy-done.5, bf16[3,2,64,2048]{3,2,1,0:T(8,128)(2,1)S(1)} %copy-done.5, bf16[1,2,64,2048]{3,2,1,0:T(8,128)(2,1)S(1)} %copy-done.9, f32[2,64,2048]{2,1,0:T(8,128)S(1)} %copy-done.19, f32[2,8,2048]{2,1,0:T(8,128)S(1)} %get-tuple-element.40.lse_ref), custom_call_target="tpu_custom_call" | custom-call | flops 22000001024 | bytes 5000000 | tf_op jit(solution)/shard_map/mixer_attend_back/pallas_call | solution.py:814
  211.2 21.3 %exchange.7 = bf16[3,8,64,512]{3,2,1,0:T(8,128)(2,1)} custom-call(bf16[3,2,64,2048]{3,2,1,0:T(8,128)(2,1)} %copy-done.6), custom_call_target="tpu_custom_call" | custom-call | tf_op jit(solution)/shard_map/exchange/pallas_call | solution.py:682
  232.5 3.6 multiply_reduce_fusion.2
  236.8 1.5 copy-done.40
  238.3 1.9 convolution_convert_fusion.1
  240.3 2.5 pad_maximum_fusion
  242.9 6.5 %fusion.6 = bf16[512,2048]{1,0:T(8,128)(2,1)S(1)} fusion(f32[512,2048]{1,0:T(8,128)} %copy-done.39, bf16[2048,512]{1,0:T(8,128)(2,1)} %param.35, f32[512,512]{1,0:T(8,128)} %copy-done.42), kind=kOutput, calls=%fused_computation.10 | convolution fusion | flops 1094975488 | bytes 9437184 | tf_op jit(solution)/shard_map/dot_general | solution.py:51
  249.9 1.5 multiply_reduce_fusion.1
  254.4 41.4 %share_grads.1 = (bf16[8,2,256,512]{3,2,1,0:T(8,128)(2,1)}, f32[8,2,8,256]{3,2,1,0:T(8,128)}) custom-call(bf16[2,256,512]{2,1,0:T(8,128)(2,1)} %bitcast.84, f32[2,8,256]{2,1,0:T(8,128)} %maximum_maximum_fusion.stat_ref), custom_call_target="tpu_custom_call" | custom-call | tf_op jit(solution)/shard_map/share_grads/pallas_call | solution.py:721
  295.8 45.4 %cross_backward.1 = (bf16[8,2,512,256]{3,2,1,0:T(8,128)(2,1)}, f32[1,2,1024,512]{3,2,1,0:T(8,128)}, f32[512,512]{1,0:T(8,128)}, f32[512,512]{1,0:T(8,128)}, f32[1,512]{1,0:T(1,128)}) custom-call(bf16[1,2,1024,512]{3,2,1,0:T(8,128)(2,1)} %tok_ref.3, f32[1,512]{1,0:T(1,128)} %bitcast.76, bf16[512,512]{1,0:T(8,128)(2,1)} %kw_ref.3, bf16[512,512]{1,0:T(8,128)(2,1)} %vw_ref.3, ...), custom_call_target="tpu_custom_call" | custom-call | flops 25999998976 | bytes 24000000 | tf_op jit(solution)/shard_map/cross_backward/pallas_call | solution.py:893
  341.3 2.2 copy-done.2
  343.5 29.0 %query_grad_sum.1 = f32[2,256,512]{2,1,0:T(8,128)S(1)} custom-call(bf16[8,2,512,256]{3,2,1,0:T(8,128)(2,1)S(1)} %copy-done.2), custom_call_target="tpu_custom_call" | custom-call | tf_op jit(solution)/shard_map/query_grad_sum/pallas_call | solution.py:630
  372.6 1.6 multiply_reduce_fusion
  374.4 4.5 fusion.16
  380.3 2.5 fusion.14
  382.8 2.8 fusion.15
  385.6 1.4 fusion.18
  391.1 72.6 %reduce-scatter.3.cloned.1.call-done = bf16[64,8320]{1,0:T(8,128)(2,1)} async-done(((bf16[512,8320]{1,0:T(8,128)(2,1)}), bf16[64,8320]{1,0:T(8,128)(2,1)}) %reduce-scatter.3.cloned.1.call-update) | async-done | bytes 1064976 | tf_op jit(solution)/shard_map/reduce_scatter | solution.py:939
  463.7 1.9 fusion.41
  466.8 2.5 convolution_add_fusion.2
  469.3 67.3 %all-reduce.5.cloned.1.call-done = (bf16[256,1024]{0,1:T(8,128)(2,1)}, bf16[64,8320]{1,0:T(8,128)(2,1)}) async-done(((bf16[256,1024]{0,1:T(8,128)(2,1)}, bf16[64,8320]{1,0:T(8,128)(2,1)}), (bf16[256,1024]{0,1:T(8,128)(2,1)}, bf16[64,8320]{1,0:T(8,128)(2,1)})) %all-reduce.5.cloned.1.call-update) | async-done | bytes 1589264 | tf_op jit(solution)/shard_map/psum | solution.py:941
  536.6 1.8 slice.80
  538.4 1.8 fusion.47
  540.2 2.3 fusion.46
  542.5 1.5 convert_element_type.104
  546.1 1.8 slice_reduce_fusion
  (203 shorter events, 27.3 us)
Async XLA Ops:
  7.2 154.8 %copy-start = (bf16[512,2048]{1,0:T(8,128)(2,1)S(1)}, bf16[512,2048]{1,0:T(8,128)(2,1)}, u32[]{:S(2)}) copy-start(bf16[512,2048]{1,0:T(8,128)(2,1)} %param.40) | copy-start | bytes 6291460
  7.2 7.7 %copy-start.14 = (bf16[512,512]{1,0:T(8,128)(2,1)S(1)}, bf16[512,512]{1,0:T(8,128)(2,1)}, u32[]{:S(2)}) copy-start(bf16[512,512]{1,0:T(8,128)(2,1)} %kw_ref.3) | copy-start | bytes 1572868
  7.2 7.7 %copy-start.11 = (bf16[512,512]{1,0:T(8,128)(2,1)S(1)}, bf16[512,512]{1,0:T(8,128)(2,1)}, u32[]{:S(2)}) copy-start(bf16[512,512]{1,0:T(8,128)(2,1)} %qw_ref.1) | copy-start | bytes 1572868
  7.2 7.7 %copy-start.13 = (f32[512]{0:T(512)S(1)}, f32[512]{0:T(512)}, u32[]{:S(2)}) copy-start(f32[512]{0:T(512)} %param.28) | copy-start | bytes 6148
  7.2 7.7 %copy-start.16 = (f32[512]{0:T(512)S(1)}, f32[512]{0:T(512)}, u32[]{:S(2)}) copy-start(f32[512]{0:T(512)} %param.27) | copy-start | bytes 6148
  7.3 383.8 %reduce-scatter.5.cloned.1.call-start = ((), (), s32[]{:S(2)}) async-start(), calls=%async_computation.3 | async-start | bytes 4718592 | tf_op jit(solution)/shard_map/reduce_scatter | solution.py:940
  13.0 39.9 %copy-start.7 = (bf16[2,1024,128]{2,1,0:T(8,128)(2,1)}, bf16[2,1024,128]{2,1,0:T(8,128)(2,1)S(1)}, u32[]{:S(2)}) copy-start(bf16[2,1024,128]{2,1,0:T(8,128)(2,1)S(1)} %fusion.22.hot_ref) | copy-start | bytes 1572868
  14.6 73.5 %copy-start.20 = (f32[1,2,256,512]{3,2,1,0:T(8,128)}, f32[1,2,256,512]{3,2,1,0:T(8,128)S(1)}, u32[]{:S(2)}) copy-start(f32[1,2,256,512]{3,2,1,0:T(8,128)S(1)} %get-tuple-element.142) | copy-start | bytes 3145732
  16.0 36.8 %copy-start.8 = (bf16[2,8,128,128]{3,2,1,0:T(8,128)(2,1)}, bf16[2,8,128,128]{3,2,1,0:T(8,128)(2,1)S(1)}, u32[]{:S(2)}) copy-start(bf16[2,8,128,128]{3,2,1,0:T(8,128)(2,1)S(1)} %broadcast_in_dim.26.tab_ref) | copy-start | bytes 1572868
  16.0 72.0 %copy-start.54 = (bf16[512,512]{1,0:T(8,128)(2,1)S(1)}, bf16[512,512]{1,0:T(8,128)(2,1)}, u32[]{:S(2)}) copy-start(bf16[512,512]{1,0:T(8,128)(2,1)} %param.32) | copy-start | bytes 1572868
  56.5 32.4 %copy-start.45 = (bf16[512,2048]{1,0:T(8,128)(2,1)S(1)}, bf16[512,2048]{1,0:T(8,128)(2,1)}, u32[]{:S(2)}) copy-start(bf16[512,2048]{1,0:T(8,128)(2,1)} %param.34) | copy-start | bytes 6291460
  56.5 32.5 %copy-start.61 = (f32[512]{0:T(512)S(1)}, f32[512]{0:T(512)}, u32[]{:S(2)}) copy-start(f32[512]{0:T(512)} %param.33) | copy-start | bytes 6148
  90.6 3.0 copy-start.56
  90.6 3.0 copy-start.60
  96.4 3.6 copy-start.64
  158.1 2.6 copy-start.44
  158.1 2.6 copy-start.50
  160.4 10.3 %copy-start.33 = (f32[512,512]{1,0:T(8,128)}, f32[512,512]{1,0:T(8,128)S(1)}, u32[]{:S(2)}) copy-start(f32[512,512]{1,0:T(8,128)S(1)} %get-tuple-element.167) | copy-start | bytes 3145732
  165.7 3.5 copy-start.69
  165.7 3.4 copy-start.68
  170.7 12.2 %copy-start.5 = (bf16[3,2,64,2048]{3,2,1,0:T(8,128)(2,1)S(1)}, bf16[3,2,64,2048]{3,2,1,0:T(8,128)(2,1)}, u32[]{:S(2)}) copy-start(bf16[3,2,64,2048]{3,2,1,0:T(8,128)(2,1)} %exchange.4.all_ref.q_ref) | copy-start | bytes 4718596
  232.5 3.6 copy-start.23
  232.5 4.1 copy-start.29
  242.8 6.7 %copy-start.21 = (f32[1,2,256,512]{3,2,1,0:T(8,128)S(1)}, f32[1,2,256,512]{3,2,1,0:T(8,128)}, u32[]{:S(2)}) copy-start(f32[1,2,256,512]{3,2,1,0:T(8,128)} %copy-done.20) | copy-start | bytes 3145732
  242.8 7.0 %copy-start.26 = (f32[512,512]{1,0:T(8,128)S(1)}, f32[512,512]{1,0:T(8,128)}, u32[]{:S(2)}) copy-start(f32[512,512]{1,0:T(8,128)} %copy-done.25) | copy-start | bytes 3145732
  242.9 220.8 %reduce-scatter.3.cloned.1.call-start = ((), (), s32[]{:S(2)}) async-start(), calls=%async_computation.2 | async-start | bytes 9584640 | tf_op jit(solution)/shard_map/reduce_scatter | solution.py:939
  242.9 6.9 %copy-start.46 = (bf16[512,2048]{1,0:T(8,128)(2,1)S(1)}, bf16[512,2048]{1,0:T(8,128)(2,1)}, u32[]{:S(2)}) copy-start(bf16[512,2048]{1,0:T(8,128)(2,1)} %param.34) | copy-start | bytes 6291460
  252.5 88.8 %copy-start.31 = (f32[512,512]{1,0:T(8,128)}, f32[512,512]{1,0:T(8,128)S(1)}, u32[]{:S(2)}) copy-start(f32[512,512]{1,0:T(8,128)S(1)} %add_add_fusion.5) | copy-start | bytes 3145732
  343.5 29.1 %copy-start.12 = (bf16[512,512]{1,0:T(8,128)(2,1)S(1)}, bf16[512,512]{1,0:T(8,128)(2,1)}, u32[]{:S(2)}) copy-start(bf16[512,512]{1,0:T(8,128)(2,1)} %qw_ref.1) | copy-start | bytes 1572868
  343.5 30.7 %copy-start.62 = (f32[1,512]{1,0:T(1,128)S(1)}, f32[1,512]{1,0:T(1,128)}, u32[]{:S(2)}) copy-start(f32[1,512]{1,0:T(1,128)} %get-tuple-element.51) | copy-start | bytes 6148
  343.5 30.9 %copy-start.34 = (f32[512,512]{1,0:T(8,128)S(1)}, f32[512,512]{1,0:T(8,128)}, u32[]{:S(2)}) copy-start(f32[512,512]{1,0:T(8,128)} %copy-done.33) | copy-start | bytes 3145732
  374.1 4.8 copy-start.30
  374.4 4.6 copy-start.38
  374.4 5.9 %copy-start.24 = (f32[512,512]{1,0:T(8,128)S(1)}, f32[512,512]{1,0:T(8,128)}, u32[]{:S(2)}) copy-start(f32[512,512]{1,0:T(8,128)} %copy-done.22) | copy-start | bytes 3145732
  374.4 5.9 %copy-start.57 = (bf16[3,8,64,512]{3,2,1,0:T(8,128)(2,1)S(1)}, bf16[3,8,64,512]{3,2,1,0:T(8,128)(2,1)}, u32[]{:S(2)}) copy-start(bf16[3,8,64,512]{3,2,1,0:T(8,128)(2,1)} %exchange.7) | copy-start | bytes 4718596
  378.9 3.8 copy-start.27
  379.0 3.8 copy-start.67
  382.7 2.8 copy-start.32
  382.7 2.8 copy-start.37
  382.8 4.2 copy-start.59
  382.8 5.1 copy-start.58
  385.6 3.4 copy-start.48
  391.0 145.6 %all-reduce.5.cloned.1.call-start = ((), (), s32[]{:S(2)}) async-start(), calls=%async_computation.4 | async-start | bytes 3178496 | tf_op jit(solution)/shard_map/psum | solution.py:941
  463.7 3.1 copy-start.51
  463.7 3.1 copy-start.70
  536.6 5.9 %copy-start.35 = (bf16[64,8320]{1,0:T(8,128)(2,1)S(1)}, bf16[64,8320]{1,0:T(8,128)(2,1)}, u32[]{:S(2)}) copy-start(bf16[64,8320]{1,0:T(8,128)(2,1)} %get-tuple-element.138) | copy-start | bytes 3194884
  536.6 7.4 %copy-start.49 = (bf16[256,1024]{0,1:T(8,128)(2,1)S(1)}, bf16[256,1024]{0,1:T(8,128)(2,1)}, u32[]{:S(2)}) copy-start(bf16[256,1024]{0,1:T(8,128)(2,1)} %get-tuple-element.137) | copy-start | bytes 1572868
  540.2 7.6 %copy-start.1 = (bf16[512,2048]{1,0:T(8,128)(2,1)S(1)}, bf16[512,2048]{1,0:T(8,128)(2,1)}, u32[]{:S(2)}) copy-start(bf16[512,2048]{1,0:T(8,128)(2,1)} %param.40) | copy-start | bytes 6291460
  (26 other events, 39.7 us)
Sparse Core Ops, SparseCore 0:
  243.0 65.0 reduce-scatter.4
  391.1 72.4 reduce-scatter.2
  466.2 70.3 all-reduce.4

commit v2 on v1

--- a/solution.py
+++ b/solution.py
@@ -935,10 +935,142 @@
     )(tokens, token_gain, key_weight, value_weight, hot, table, keys, values, queries, upstream, stats)
 
 
-def reduce_grads(columns, rows):
-    part = lax.psum_scatter(columns.astype(BF16), "tok", scatter_dimension=0, tiled=True)
-    other = lax.psum_scatter(rows.astype(BF16), "tok", scatter_dimension=0, tiled=True)
-    return lax.psum((part, other), "grp")
+def reduce_kernel(items, *refs):
+    n = len(items)
+    sources, outs, scratch = refs[:n], refs[n:2 * n], refs[2 * n:]
+    mine, got, first_in, second_in, z_keep, z_first, z_second = [scratch[i * n:(i + 1) * n] for i in range(7)]
+    (local_sem, core_send, core_recv, one_send, one_recv, two_send, two_recv, z_send, z_recv) = scratch[7 * n:]
+    me, core, chip, mate, (far, flip_x, flip_y) = places()
+    targets = (chip, flip_x, flip_y, far)
+    level = lax.axis_index("grp")
+    odd = lax.rem(level, 2)
+    level_near = level + 1 - 2 * odd
+    level_far = lax.rem(level + 2, 4)
+    barrier = pltpu.get_barrier_semaphore()
+    for device in (mate, 2 * flip_x + core, 2 * flip_y + core):
+        pl.semaphore_signal(barrier, inc=1, device_id={"tok": device}, device_id_type=pl.DeviceIdType.MESH)
+    for other in (level_near, level_far):
+        pl.semaphore_signal(barrier, inc=1, device_id={"grp": other}, device_id_type=pl.DeviceIdType.MESH)
+    pl.semaphore_wait(barrier, 5)
+
+    def along(item, src, dst, step, other):
+        return pltpu.make_async_remote_copy(
+            src_ref=src, dst_ref=dst, send_sem=z_send.at[item, step], recv_sem=z_recv.at[item, step],
+            device_id={"grp": other}, device_id_type=pl.DeviceIdType.MESH,
+        )
+
+    sent, cores, ones, twos, zs = [], {}, {}, {}, {}
+    for i, (rows, columns, kind, x_first) in enumerate(items):
+        cores[i] = []
+        for slot in (3, 2, 1, 0):
+            own_rows = pl.ds(pl.multiple_of((2 * targets[slot] + core) * rows, rows), rows)
+            mate_rows = pl.ds(pl.multiple_of((2 * targets[slot] + 1 - core) * rows, rows), rows)
+            there = remote(sources[i].at[mate_rows], got[i].at[slot], core_send.at[i, slot], core_recv.at[i, slot], mate)
+            here = pltpu.make_async_copy(sources[i].at[own_rows], mine[i].at[slot], local_sem.at[i, slot])
+            there.start()
+            here.start()
+            cores[i].append((slot, there, here))
+            sent.append(there)
+
+    def add(target, one, two, kind):
+        target[...] = (one[...].astype(F32) + two[...].astype(F32)).astype(kind)
+
+    def core_sums(i):
+        rows, columns, kind, x_first = items[i]
+        for slot, there, here in cores[i]:
+            there.wait_recv()
+            here.wait()
+            add(mine[i].at[slot], mine[i].at[slot], got[i].at[slot], kind)
+        near = 1 if x_first else 2
+        peer = 2 * targets[near] + core
+        ones[i] = []
+        for place, slot in ((1, 3), (0, near)):
+            copy = remote(mine[i].at[slot], first_in[i].at[place], one_send.at[i, place], one_recv.at[i, place], peer)
+            copy.start()
+            ones[i].append((place, copy))
+            sent.append(copy)
+
+    def first_sums(i):
+        rows, columns, kind, x_first = items[i]
+        other = 2 if x_first else 1
+        for place, copy in ones[i]:
+            copy.wait_recv()
+            slot = other if place == 1 else 0
+            add(mine[i].at[slot], mine[i].at[slot], first_in[i].at[place], kind)
+            if place == 1:
+                twos[i] = remote(mine[i].at[slot], second_in[i], two_send.at[i], two_recv.at[i], 2 * targets[other] + core)
+                twos[i].start()
+                sent.append(twos[i])
+
+    def second_sums(i):
+        rows, columns, kind, x_first = items[i]
+        half = rows // 2
+        twos[i].wait_recv()
+        add(mine[i].at[0], mine[i].at[0], second_in[i], kind)
+        away = pl.ds(pl.multiple_of((1 - odd) * half, half), half)
+        zs[i, 0] = along(i, mine[i].at[0, away], z_first[i], 0, level_near)
+        zs[i, 0].start()
+        sent.append(zs[i, 0])
+
+    def grp_first(i):
+        rows, columns, kind, x_first = items[i]
+        half = rows // 2
+        keep = pl.ds(pl.multiple_of(odd * half, half), half)
+        zs[i, 0].wait_recv()
+        add(z_keep[i].at[0], mine[i].at[0, keep], z_first[i], kind)
+        zs[i, 1] = along(i, z_keep[i].at[0], z_second[i].at[0], 1, level_far)
+        zs[i, 1].start()
+        sent.append(zs[i, 1])
+
+    def grp_second(i):
+        rows, columns, kind, x_first = items[i]
+        half = rows // 2
+        keep = pl.ds(pl.multiple_of(odd * half, half), half)
+        zs[i, 1].wait_recv()
+        add(z_keep[i].at[1], z_keep[i].at[0], z_second[i].at[0], kind)
+        zs[i, 2] = along(i, z_keep[i].at[1], z_second[i].at[1], 2, level_near)
+        zs[i, 2].start()
+        sent.append(zs[i, 2])
+        outs[i][keep] = z_keep[i][1].astype(F32)
+
+    def grp_third(i):
+        rows, columns, kind, x_first = items[i]
+        half = rows // 2
+        away = pl.ds(pl.multiple_of((1 - odd) * half, half), half)
+        zs[i, 2].wait_recv()
+        outs[i][away] = z_second[i][1].astype(F32)
+
+    stages = (core_sums, first_sums, second_sums, grp_first, grp_second, grp_third)
+    lags = (0, 2, 3, 4, 5, 6)
+    for step in range(n + lags[-1]):
+        for stage, lag in zip(stages, lags):
+            if 0 <= step - lag < n:
+                stage(step - lag)
+    for copy in sent:
+        copy.wait_send()
+
+
+def reduce_grads(collective_id, arrays, x_firsts):
+    items = tuple(
+        (array.shape[0] // TOK, array.shape[1], array.dtype, x_first) for array, x_first in zip(arrays, x_firsts)
+    )
+    n = len(items)
+    dma = pltpu.SemaphoreType.DMA
+    blocks = lambda count, part: [
+        pltpu.VMEM(((count,) if count else ()) + (rows // part, columns), kind) for rows, columns, kind, unused in items
+    ]
+    return pl.pallas_call(
+        functools.partial(reduce_kernel, items),
+        in_specs=[pl.BlockSpec(memory_space=pl.ANY)] * n,
+        out_specs=[pl.BlockSpec(memory_space=pltpu.VMEM)] * n,
+        out_shape=[jax.ShapeDtypeStruct((rows, columns), F32) for rows, columns, kind, unused in items],
+        scratch_shapes=blocks(4, 1) + blocks(4, 1) + blocks(2, 1) + blocks(0, 1) + blocks(2, 2) + blocks(0, 2) + blocks(2, 2)
+        + [dma((n, 4)), dma((n, 4)), dma((n, 4)), dma((n, 2)), dma((n, 2)), dma((n,)), dma((n,)), dma((n, 3)), dma((n, 3))],
+        compiler_params=pltpu.CompilerParams(
+            collective_id=collective_id, has_side_effects=True, vmem_limit_bytes=56 * MIB
+        ),
+        name="reduce_grads",
+    )(*arrays)
 
 
 def fast_body(
@@ -1032,39 +1164,40 @@
     latent_grad, d_query_gain = norm_back(latent_in, query_gain, nt(query_grad, query_weight))
     latent_grad = upstream + latent_grad
 
-    columns, rows = reduce_grads(
-        jnp.concatenate(
-            [d_second_up, d_mixer_output, d_mixer_project, d_first_up, d_output, d_key, d_value, d_query,
-             jnp.pad(jnp.stack([d_second_gain, d_mixer_gain, d_first_gain, d_token_gain[0], d_query_gain], axis=1), ((0, 0), (0, 123)))], axis=1
-        ),
-        jnp.concatenate([d_second_down, d_first_down], axis=1),
-    )
-    columns = columns.astype(F32)
-    rows = rows.astype(F32)
-    widths = [FF, D, 3 * D, FF, D, D, D, D, 128]
-    cuts = [sum(widths[:i]) for i in range(len(widths) + 1)]
-    (o_second_up, o_mixer_output, o_mixer_project, o_first_up, o_output, o_key, o_value, o_query, o_gains) = [
-        columns[:, cuts[i]:cuts[i + 1]] for i in range(len(widths))
-    ]
+    small = jnp.concatenate(
+        [d.astype(BF16) for d in (d_mixer_output, d_output, d_key, d_value, d_query)], axis=1
+    )
+    gains = jnp.stack([d_token_gain[0], d_query_gain, d_first_gain, d_mixer_gain, d_second_gain])
+    gains = jnp.pad(
+        gains.reshape(5, TOK, D // TOK).transpose(1, 0, 2), ((0, 0), (0, 11), (0, 128 - D // TOK))
+    ).reshape(TOK * 16, 128)
+    o_second_down, o_second_up, o_first_down, o_first_up, o_project, o_small, o_gains = reduce_grads(
+        7,
+        [d_second_down.astype(BF16), d_second_up.astype(BF16), d_first_down.astype(BF16),
+         d_first_up.astype(BF16), d_mixer_project.astype(BF16), small, gains],
+        (False, True, False, True, True, False, False),
+    )
+    o_mixer_output, o_output, o_key, o_value, o_query = [o_small[:, i * D:(i + 1) * D] for i in range(5)]
+    o_gains = o_gains[:, :D // TOK]
     return (
         final_rows.reshape(1, MB, ROWS, D),
         latent_grad.reshape(1, MB, ROWS, D),
         tokens_grad,
-        o_gains[:, 3],
-        o_gains[:, 4],
+        o_gains[0],
+        o_gains[1],
         o_query,
         o_key,
         o_value,
         o_output,
-        o_gains[:, 2],
+        o_gains[2],
         o_first_up,
-        rows[:, D:],
-        o_gains[:, 1],
-        o_mixer_project,
+        o_first_down,
+        o_gains[3],
+        o_project,
         o_mixer_output,
-        o_gains[:, 0],
+        o_gains[4],
         o_second_up,
-        rows[:, :D],
+        o_second_down,
     )
 
 

time: 564 us -> 501 us (0.89)
  waiting for transfers between devices: 140 us -> 0 us
  Pallas kernels: 291 us -> 379 us
  between operations: 14.9 us -> 1.86 us
    pallas_call x0 -> x1, Pallas kernels: none -> 99.8 us  [reduce_grads(): pl.pallas_call(functools.partial(reduce_kernel, items), in_specs=[pl.Bloc...]
    reduce_scatter x2 -> x0, waiting for transfers between devices: 72.6 us -> none  [the longest x1 72.6 us: reduce_grads(): lax.psum_scatter(columns.astype(BF16), 'tok', scatter_dimension=0, tiled=...]
    psum x1 -> x0, waiting for transfers between devices: 67.3 us -> none  [reduce_grads(): return lax.psum((part, other), 'grp')]
    pallas_call x1, Pallas kernels: 41.4 us -> 30.2 us  [share(): pl.pallas_call(share_kernel, in_specs=[pl.BlockSpec(memory_space=pl.ANY)]...]
    slice x5 -> x1, local copies, waits for them, and re-layouts: 7.73 us -> 2 us  [fast_body(): o_small[:, i * D:(i + 1) * D]]
    unnamed x146 -> x129, local copies, waits for them, and re-layouts: 20 us -> 23 us
  transfers between devices with their start and end apart: 3 -> 0, of which waited for: 2 -> 0; matrix products, arithmetic and copies ran while one was open for 6% -> 0% of each run, Pallas kernels for 21% -> 0%
where the time goes in v2:
time: 501 us; the launch traced here: 492 us
  Pallas kernels  379 us (76%)
  matrix products  54.9 us (11%)
  local copies, waits for them, and re-layouts  33.8 us (7%)
  other arithmetic  22.3 us (4%)
    pallas_call x1, Pallas kernels, reduce_grads(): pl.pallas_call(functools.partial(reduce_kernel, items), in_specs=[pl.Bloc...  99.8 us
    pallas_call x4, Pallas kernels, exchange(): pl.pallas_call(functools.partial(exchange_kernel, to_heads), in_specs=[pl...  61.3 us
    pallas_call x2, Pallas kernels, gather_sum(): pl.pallas_call(functools.partial(gather_sum_kernel, softmax), in_specs=[p...  60.5 us
    pallas_call x1, Pallas kernels, cross_backward(): pl.pallas_call(cross_backward_kernel, grid=(MB, LGROUPS), in_specs=[pl.Bl...  45.3 us
    pallas_call x1, Pallas kernels, cross_forward(): pl.pallas_call(cross_forward_kernel, grid=(MB, LGROUPS), in_specs=[pl.Blo...  36.9 us
    pallas_call x1, Pallas kernels, share(): pl.pallas_call(share_kernel, in_specs=[pl.BlockSpec(memory_space=pl.ANY)]...  30.2 us
    pallas_call x1, Pallas kernels, mixer_attend_back(): pl.pallas_call(mixer_attend_back_kernel, grid=(MB, L // QB), in_specs=[pl...  24.7 us
    unnamed x129, local copies, waits for them, and re-layouts  23 us

profile of v2, /device:TPU:0, one launch (start us, length us, event | category | flops | bytes accessed | tf_op | source)
XLA Modules:
  0.0 491.7 jit_solution(1652719504704480663)
XLA Ops:
  2.8 2.3 fusion.19.hot_ref
  5.1 1.5 bitcast_convert_fusion
  6.6 1.6 fusion.39
  11.3 3.3 fusion.47
  14.7 36.9 %cross_forward.1 = (bf16[2,1024,512]{2,1,0:T(8,128)(2,1)S(1)}, bf16[2,1024,512]{2,1,0:T(8,128)(2,1)}, bf16[2,2048,512]{2,1,0:T(8,128)(2,1)}, bf16[8,2,512,256]{3,2,1,0:T(8,128)(2,1)}, f32[8,2,8,256]{3,2,1,0:T(8,128)S(1)}) custom-call(bf16[1,2,1024,512]{3,2,1,0:T(8,128)(2,1)} %tok_ref.3, f32[1,2,2048,512]{3,2,1,0:T(8,128)} %lat_ref.1, f32[1,512]{1,0:T(1,128)S(1)} %bitcast.88, ...), custom_call_target="tpu_custom_call" | custom-call | flops 14000000000 | bytes 22000000 | tf_op jit(solution)/shard_map/cross_forward/pallas_call | solution.py:490
  51.5 1.4 copy-done.17
  52.9 2.2 copy-done.3
  55.1 31.5 %weighted_sum.1 = (f32[2,256,512]{2,1,0:T(8,128)S(1)}, f32[2,8,256]{2,1,0:T(8,128)S(1)}) custom-call(bf16[8,2,512,256]{3,2,1,0:T(8,128)(2,1)S(1)} %copy-done.3, f32[8,2,8,256]{3,2,1,0:T(8,128)S(1)} %get-tuple-element.43.refs_1_), custom_call_target="tpu_custom_call" | custom-call | tf_op jit(solution)/shard_map/weighted_sum/pallas_call | solution.py:630
  87.6 1.3 fusion.36
  89.2 1.6 fusion.45
  92.2 2.8 convolution_bitcast_fusion
  95.0 4.0 copy.47
  99.1 3.6 multiply_convert_fusion.2.src_ref
  102.7 20.9 %exchange.4.all_ref.q_ref = bf16[3,2,64,2048]{3,2,1,0:T(8,128)(2,1)} custom-call(bf16[3,8,64,512]{3,2,1,0:T(8,128)(2,1)} %multiply_convert_fusion.2.src_ref), custom_call_target="tpu_custom_call" | custom-call | tf_op jit(solution)/shard_map/exchange/pallas_call | solution.py:682
  123.6 1.4 copy-done.4
  125.0 20.4 %mixer_attend.1 = (bf16[1,2,64,2048]{3,2,1,0:T(8,128)(2,1)S(1)}, f32[2,64,2048]{2,1,0:T(8,128)S(1)}, f32[2,8,2048]{2,1,0:T(8,128)S(1)}) custom-call(bf16[3,2,64,2048]{3,2,1,0:T(8,128)(2,1)S(1)} %copy-done.4, bf16[3,2,64,2048]{3,2,1,0:T(8,128)(2,1)S(1)} %copy-done.4), custom_call_target="tpu_custom_call" | custom-call | flops 8999999488 | bytes 4000000 | tf_op jit(solution)/shard_map/mixer_attend/pallas_call | solution.py:758
  147.1 9.9 %exchange.5 = bf16[1,8,64,512]{3,2,1,0:T(8,128)(2,1)} custom-call(bf16[1,2,64,2048]{3,2,1,0:T(8,128)(2,1)} %copy-done.10), custom_call_target="tpu_custom_call" | custom-call | tf_op jit(solution)/shard_map/exchange/pallas_call | solution.py:682
  157.1 2.2 fusion.46
  159.9 3.7 fusion.13
  163.6 2.5 convolution_add_fusion.2
  166.1 3.2 convolution_convert_fusion.4.refs_0_
  169.3 1.6 multiply_reduce_fusion
  170.9 2.8 convolution_convert_fusion.3.refs_1_
  175.6 2.5 convolution_convert_fusion.9
  178.0 9.2 %exchange.6.up_ref = bf16[1,2,64,2048]{3,2,1,0:T(8,128)(2,1)} custom-call(bf16[1,8,64,512]{3,2,1,0:T(8,128)(2,1)} %bitcast.96), custom_call_target="tpu_custom_call" | custom-call | tf_op jit(solution)/shard_map/exchange/pallas_call | solution.py:682
  189.5 24.7 %mixer_attend_back.1.src_ref = bf16[3,2,64,2048]{3,2,1,0:T(8,128)(2,1)S(1)} custom-call(bf16[3,2,64,2048]{3,2,1,0:T(8,128)(2,1)S(1)} %copy-done.5, bf16[3,2,64,2048]{3,2,1,0:T(8,128)(2,1)S(1)} %copy-done.5, bf16[1,2,64,2048]{3,2,1,0:T(8,128)(2,1)S(1)} %copy-done.9, f32[2,64,2048]{2,1,0:T(8,128)S(1)} %copy-done.19, f32[2,8,2048]{2,1,0:T(8,128)S(1)} %get-tuple-element.47.lse_ref), custom_call_target="tpu_custom_call" | custom-call | flops 22000001024 | bytes 5000000 | tf_op jit(solution)/shard_map/mixer_attend_back/pallas_call | solution.py:814
  215.4 21.3 %exchange.7 = bf16[3,8,64,512]{3,2,1,0:T(8,128)(2,1)} custom-call(bf16[3,2,64,2048]{3,2,1,0:T(8,128)(2,1)} %copy-done.6), custom_call_target="tpu_custom_call" | custom-call | tf_op jit(solution)/shard_map/exchange/pallas_call | solution.py:682
  236.7 3.6 multiply_reduce_fusion.1
  240.3 2.5 convolution_convert_fusion.refs_4_
  243.5 2.7 fusion.14
  246.2 6.1 %fusion.6 = bf16[512,2048]{1,0:T(8,128)(2,1)S(1)} fusion(f32[512,2048]{1,0:T(8,128)} %copy-done.32, bf16[2048,512]{1,0:T(8,128)(2,1)} %param.35, f32[512,512]{1,0:T(8,128)S(1)} %add_add_fusion.6), kind=kOutput, calls=%fused_computation.10 | convolution fusion | flops 1094975488 | bytes 9437184 | tf_op jit(solution)/shard_map/dot_general | solution.py:51
  252.3 3.3 convolution_convert_fusion.2.refs_2_
  255.6 1.5 multiply_reduce_fusion.2
  257.1 2.8 convolution_convert_fusion.1.refs_3_
  261.0 1.3 fusion.15
  264.3 30.2 %share_grads.1 = (bf16[8,2,256,512]{3,2,1,0:T(8,128)(2,1)}, f32[8,2,8,256]{3,2,1,0:T(8,128)}) custom-call(bf16[2,256,512]{2,1,0:T(8,128)(2,1)} %bitcast.95, f32[2,8,256]{2,1,0:T(8,128)} %maximum_maximum_fusion.stat_ref), custom_call_target="tpu_custom_call" | custom-call | tf_op jit(solution)/shard_map/share_grads/pallas_call | solution.py:721
  294.5 45.3 %cross_backward.1 = (bf16[8,2,512,256]{3,2,1,0:T(8,128)(2,1)}, f32[1,2,1024,512]{3,2,1,0:T(8,128)}, f32[512,512]{1,0:T(8,128)}, f32[512,512]{1,0:T(8,128)}, f32[1,512]{1,0:T(1,128)}) custom-call(bf16[1,2,1024,512]{3,2,1,0:T(8,128)(2,1)} %tok_ref.3, f32[1,512]{1,0:T(1,128)} %bitcast.87, bf16[512,512]{1,0:T(8,128)(2,1)} %kw_ref.3, bf16[512,512]{1,0:T(8,128)(2,1)} %vw_ref.3, ...), custom_call_target="tpu_custom_call" | custom-call | flops 25999998976 | bytes 24000000 | tf_op jit(solution)/shard_map/cross_backward/pallas_call | solution.py:893
  339.8 2.1 convert_dynamic-update-slice_fusion.1
  341.9 2.2 convert_dynamic-update-slice_fusion
  344.1 2.2 copy-done.2
  346.3 29.0 %query_grad_sum.1 = f32[2,256,512]{2,1,0:T(8,128)S(1)} custom-call(bf16[8,2,512,256]{3,2,1,0:T(8,128)(2,1)S(1)} %copy-done.2), custom_call_target="tpu_custom_call" | custom-call | tf_op jit(solution)/shard_map/query_grad_sum/pallas_call | solution.py:630
  375.4 1.3 fusion.16.refs_5_
  381.0 99.8 %reduce_grads.1 = (f32[256,512]{1,0:T(8,128)}, f32[64,2048]{1,0:T(8,128)}, f32[256,512]{1,0:T(8,128)}, f32[64,2048]{1,0:T(8,128)}, f32[64,1536]{1,0:T(8,128)}, /*index=5*/f32[64,2560]{1,0:T(8,128)}, f32[16,128]{1,0:T(8,128)}) custom-call(bf16[2048,512]{1,0:T(8,128)(2,1)} %convolution_convert_fusion.4.refs_0_, ...), custom_call_target="tpu_custom_call" | custom-call | tf_op jit(solution)/shard_map/reduce_grads/pallas_call | solution.py:1062
  480.8 1.4 slice_bitcast_fusion
  482.2 2.0 fusion.43
  484.2 1.9 copy.66
  486.1 1.9 copy.67
  487.9 1.8 copy.68
  (174 shorter events, 25.2 us)
Async XLA Ops:
  0.7 158.9 %copy-start = (bf16[512,2048]{1,0:T(8,128)(2,1)S(1)}, bf16[512,2048]{1,0:T(8,128)(2,1)}, u32[]{:S(2)}) copy-start(bf16[512,2048]{1,0:T(8,128)(2,1)} %param.40) | copy-start | bytes 6291460
  0.7 9.6 %copy-start.13 = (f32[512]{0:T(512)S(1)}, f32[512]{0:T(512)}, u32[]{:S(2)}) copy-start(f32[512]{0:T(512)} %param.28) | copy-start | bytes 6148
  2.4 8.9 %copy-start.41 = (bf16[2048,512]{1,0:T(8,128)(2,1)S(1)}, bf16[2048,512]{1,0:T(8,128)(2,1)}, u32[]{:S(2)}) copy-start(bf16[2048,512]{1,0:T(8,128)(2,1)} %param.41) | copy-start | bytes 6291460
  2.8 11.9 %copy-start.7 = (bf16[2,8,128,128]{3,2,1,0:T(8,128)(2,1)}, bf16[2,8,128,128]{3,2,1,0:T(8,128)(2,1)S(1)}, u32[]{:S(2)}) copy-start(bf16[2,8,128,128]{3,2,1,0:T(8,128)(2,1)S(1)} %broadcast_in_dim.26.tab_ref) | copy-start | bytes 1572868
  5.1 9.5 %copy-start.8 = (bf16[2,1024,128]{2,1,0:T(8,128)(2,1)}, bf16[2,1024,128]{2,1,0:T(8,128)(2,1)S(1)}, u32[]{:S(2)}) copy-start(bf16[2,1024,128]{2,1,0:T(8,128)(2,1)S(1)} %fusion.19.hot_ref) | copy-start | bytes 1572868
  6.6 4.7 copy-start.37
  8.2 78.5 %copy-start.20 = (f32[1,2,256,512]{3,2,1,0:T(8,128)}, f32[1,2,256,512]{3,2,1,0:T(8,128)S(1)}, u32[]{:S(2)}) copy-start(f32[1,2,256,512]{3,2,1,0:T(8,128)S(1)} %get-tuple-element.77) | copy-start | bytes 3145732
  11.3 3.3 copy-start.11
  11.3 3.3 copy-start.14
  11.3 3.3 copy-start.15
  11.3 3.3 copy-start.16
  14.7 72.1 %copy-start.44 = (bf16[512,512]{1,0:T(8,128)(2,1)S(1)}, bf16[512,512]{1,0:T(8,128)(2,1)}, u32[]{:S(2)}) copy-start(bf16[512,512]{1,0:T(8,128)(2,1)} %param.32) | copy-start | bytes 1572868
  52.9 2.2 copy-start.3
  55.1 32.5 %copy-start.39 = (bf16[512,2048]{1,0:T(8,128)(2,1)S(1)}, bf16[512,2048]{1,0:T(8,128)(2,1)}, u32[]{:S(2)}) copy-start(bf16[512,2048]{1,0:T(8,128)(2,1)} %param.34) | copy-start | bytes 6291460
  55.1 32.5 %copy-start.54 = (f32[512]{0:T(512)S(1)}, f32[512]{0:T(512)}, u32[]{:S(2)}) copy-start(f32[512]{0:T(512)} %param.33) | copy-start | bytes 6148
  87.3 2.0 copy-start.60
  89.2 2.0 copy-start.32
  89.2 3.0 copy-start.46
  89.2 3.0 copy-start.51
  95.0 4.1 copy-start.59
  147.1 12.5 %copy-start.58 = (f32[512]{0:T(512)S(1)}, f32[512]{0:T(512)}, u32[]{:S(2)}) copy-start(f32[512]{0:T(512)} %param.39) | copy-start | bytes 6148
  157.1 2.8 copy-start.29
  159.9 3.7 copy-start.42
  163.6 2.5 copy-start.38
  170.9 3.3 copy-start.34
  173.7 13.5 %copy-start.5 = (bf16[3,2,64,2048]{3,2,1,0:T(8,128)(2,1)S(1)}, bf16[3,2,64,2048]{3,2,1,0:T(8,128)(2,1)}, u32[]{:S(2)}) copy-start(bf16[3,2,64,2048]{3,2,1,0:T(8,128)(2,1)} %exchange.4.all_ref.q_ref) | copy-start | bytes 4718596
  236.7 3.6 copy-start.23
  236.7 3.6 copy-start.47
  240.3 2.9 copy-start.26
  243.4 8.9 %copy-start.35 = (f32[512,512]{1,0:T(8,128)}, f32[512,512]{1,0:T(8,128)S(1)}, u32[]{:S(2)}) copy-start(f32[512,512]{1,0:T(8,128)S(1)} %add_add_fusion.6) | copy-start | bytes 3145732
  246.2 6.1 %copy-start.33 = (f32[512,2048]{1,0:T(8,128)S(1)}, f32[512,2048]{1,0:T(8,128)}, u32[]{:S(2)}) copy-start(f32[512,2048]{1,0:T(8,128)} %copy-done.32) | copy-start | bytes 12582916
  252.3 3.3 copy-start.25
  252.3 3.3 copy-start.40
  257.1 3.3 copy-start.36
  259.9 2.3 copy-start.45
  261.0 78.8 %copy-start.27 = (f32[512,512]{1,0:T(8,128)}, f32[512,512]{1,0:T(8,128)S(1)}, u32[]{:S(2)}) copy-start(f32[512,512]{1,0:T(8,128)S(1)} %add_add_fusion.5) | copy-start | bytes 3145732
  341.9 33.5 %copy-start.48 = (bf16[1,2,256,512]{3,2,1,0:T(8,128)(2,1)S(1)}, bf16[1,2,256,512]{3,2,1,0:T(8,128)(2,1)}, u32[]{:S(2)}) copy-start(bf16[1,2,256,512]{3,2,1,0:T(8,128)(2,1)} %multiply_convert_fusion.3) | copy-start | bytes 1572868
  344.1 2.2 copy-start.2
  346.3 30.9 %copy-start.57 = (f32[1,512]{1,0:T(1,128)S(1)}, f32[1,512]{1,0:T(1,128)}, u32[]{:S(2)}) copy-start(f32[1,512]{1,0:T(1,128)} %get-tuple-element.58) | copy-start | bytes 6148
  346.3 31.7 %copy-start.12 = (bf16[512,512]{1,0:T(8,128)(2,1)S(1)}, bf16[512,512]{1,0:T(8,128)(2,1)}, u32[]{:S(2)}) copy-start(bf16[512,512]{1,0:T(8,128)(2,1)} %qw_ref.1) | copy-start | bytes 1572868
  346.3 31.7 %copy-start.21 = (f32[1,2,256,512]{3,2,1,0:T(8,128)S(1)}, f32[1,2,256,512]{3,2,1,0:T(8,128)}, u32[]{:S(2)}) copy-start(f32[1,2,256,512]{3,2,1,0:T(8,128)} %copy-done.20) | copy-start | bytes 3145732
  346.3 31.7 %copy-start.55 = (f32[1,2,2,128]{3,1,2,0:T(2,128)S(1)}, f32[1,2,2,128]{3,1,2,0:T(2,128)}, u32[]{:S(2)}) copy-start(f32[1,2,2,128]{3,1,2,0:T(2,128)} %copy.56) | copy-start | bytes 6148
  346.3 31.7 %copy-start.56 = (f32[512]{0:T(512)S(1)}, f32[512]{0:T(512)}, u32[]{:S(2)}) copy-start(f32[512]{0:T(512)} %rsqrt.50) | copy-start | bytes 6148
  375.3 3.3 copy-start.53
  375.4 3.7 copy-start.28
  381.0 110.3 %copy-start.1 = (bf16[512,2048]{1,0:T(8,128)(2,1)S(1)}, bf16[512,2048]{1,0:T(8,128)(2,1)}, u32[]{:S(2)}) copy-start(bf16[512,2048]{1,0:T(8,128)(2,1)} %param.40) | copy-start | bytes 6291460
  480.8 8.9 %copy-start.50 = (f32[64,2048]{1,0:T(8,128)S(1)}, f32[64,2048]{1,0:T(8,128)}, u32[]{:S(2)}) copy-start(f32[64,2048]{1,0:T(8,128)} %get-tuple-element.146) | copy-start | bytes 1572868
  480.8 9.7 %copy-start.49 = (f32[256,512]{1,0:T(8,128)S(1)}, f32[256,512]{1,0:T(8,128)}, u32[]{:S(2)}) copy-start(f32[256,512]{1,0:T(8,128)} %get-tuple-element.147) | copy-start | bytes 1572868
  (13 other events, 14.9 us)
